TPU v7x, 32 devices: a whole 2x2x4 slice. The times are simulated.
32 devices in a mesh: gx: 16 (over z, y, core), gy: 2 (over x).
Axes of the slice: x: 2, y: 2, z: 4, core: 2. Of those that a mesh axis runs over, the one named last changes fastest.
Arguments:
- state: bfloat16 [4, 2, 4096, 4096], P(None, None, 'gx', 'gy'), may hold values from -6 to 6
- heights: int32 [4096, 4096], P('gx', 'gy'), may hold values from 0 to 1
- surface_flag: int32 [4096, 4096], P('gx', 'gy'), may hold values 0 or 1
Outputs:
- tendency: bfloat16 [4, 2, 4096, 4096], P(None, None, 'gx', 'gy')
- spectrum: float32 [2, 2, 4096, 4096], P(None, None, ('gx', 'gy'))
All inputs are finite; a program needn't handle non-finite values. No bound on the sum of `surface_flag` on one device may be relied on, other than what follows from the above.
Results may differ from a plain program's by a relative error of at most 0.002.
Values may be sent and summed in bfloat16 or wider, within the bound.
A program may use at most 192 MiB of HBM per device.

v0:
```python
import math

import jax
import jax.numpy as jnp
from jax import lax
from jax.sharding import PartitionSpec as P

NU = 0.1
BETA = 0.5
HEAT = 1.0
DT = 0.5
HIGH = lax.Precision.HIGHEST


def with_halo(array, sides, width):
    for axis, dim in sides:
        count, length = (lax.axis_size(axis), array.shape[dim])
        up = [(i, (i + 1) % count) for i in range(count)]
        down = [(j, i) for i, j in up]
        last = lax.slice_in_dim(array, length - width, length, axis=dim)
        initial = lax.slice_in_dim(array, 0, width, axis=dim)
        before = lax.ppermute(last, axis, up)
        after = lax.ppermute(initial, axis, down)
        array = jnp.concatenate([before, array, after], axis=dim)
    return array


def raised(field):
    zero = jnp.zeros_like(field[:1])
    return jnp.concatenate([field[1:], zero], axis=0)


def lowered(field):
    zero = jnp.zeros_like(field[:1])
    return jnp.concatenate([zero, field[:-1]], axis=0)


def tendency_one(component, field, pick, center, fluid, surface):
    slope_x = (
        45.0 * (pick(1, 0) - pick(-1, 0))
        - 9.0 * (pick(2, 0) - pick(-2, 0))
        + (pick(3, 0) - pick(-3, 0))
    ) / 60.0
    slope_y = (
        45.0 * (pick(0, 1) - pick(0, -1))
        - 9.0 * (pick(0, 2) - pick(0, -2))
        + (pick(0, 3) - pick(0, -3))
    ) / 60.0
    above = raised(field)
    below = lowered(field)
    slope_z = (above - below) * 0.5
    advect = center[0] * slope_x + center[1] * slope_y + center[2] * slope_z
    spread = (
        pick(1, 0)
        + pick(-1, 0)
        + pick(0, 1)
        + pick(0, -1)
        - 4.0 * field
        + (above + below - 2.0 * field)
    )
    result = NU * spread - advect
    if component == 2:
        result = result + BETA * center[3]
    if component == 3:
        result = result + HEAT * surface
    return fluid * result


def region_tendency(padded, fluid, surface):
    rows_x = padded.shape[2]
    rows_y = padded.shape[3]
    center = padded[:, :, 3 : rows_x - 3, 3 : rows_y - 3]
    pieces = []
    for component in range(4):
        source = padded[component]

        def pick(step_x, step_y, source=source):
            return source[:, 3 + step_x : rows_x - 3 + step_x, 3 + step_y : rows_y - 3 + step_y]

        pieces.append(
            tendency_one(component, center[component], pick, center, fluid, surface).astype(
                jnp.bfloat16
            )
        )
    return jnp.stack(pieces)


def angle_table(first, second, length):
    product = first * second % length
    angle = product.astype(jnp.float32) * (2.0 * math.pi / length)
    return (jnp.cos(angle), jnp.sin(angle))


def transform_y(columns):
    levels, piece_x, length = columns.shape
    width = levels * piece_x
    outer = length // 64
    flat = columns.reshape(width, outer, 64)
    index_outer = jnp.arange(outer, dtype=jnp.int32)
    index_inner = jnp.arange(64, dtype=jnp.int32)
    cos_a, sin_a = angle_table(index_outer[:, None], index_outer[None, :], outer)
    real_a = jnp.einsum("mpl,pk->klm", flat, cos_a, precision=HIGH)
    imag_a = -jnp.einsum("mpl,pk->klm", flat, sin_a, precision=HIGH)
    cos_t, sin_t = angle_table(index_outer[:, None], index_inner[None, :], length)
    cos_t = cos_t[:, :, None]
    sin_t = sin_t[:, :, None]
    real_t = real_a * cos_t + imag_a * sin_t
    imag_t = imag_a * cos_t - real_a * sin_t
    cos_b, sin_b = angle_table(index_inner[:, None], index_inner[None, :], 64)
    real_b = jnp.einsum("klm,lj->jkm", real_t, cos_b, precision=HIGH) + jnp.einsum(
        "klm,lj->jkm", imag_t, sin_b, precision=HIGH
    )
    imag_b = jnp.einsum("klm,lj->jkm", imag_t, cos_b, precision=HIGH) - jnp.einsum(
        "klm,lj->jkm", real_t, sin_b, precision=HIGH
    )
    return jnp.stack([real_b.reshape(length, width), imag_b.reshape(length, width)])


def transform_x(moved, count_a, count_b, order, levels, scale):
    wave_rows = moved.shape[1]
    inner = moved.shape[2] // (count_a * count_b * levels)
    outer = count_a * count_b
    length = outer * inner
    parts = moved.reshape(2, wave_rows, count_a, count_b, levels, inner)
    index_outer = jnp.arange(outer, dtype=jnp.int32)
    index_inner = jnp.arange(inner, dtype=jnp.int32)
    cos_a, sin_a = angle_table(order[:, :, None], index_outer[None, None, :], outer)
    real_a = jnp.einsum("yabzl,abk->yzlk", parts[0], cos_a, precision=HIGH) + jnp.einsum(
        "yabzl,abk->yzlk", parts[1], sin_a, precision=HIGH
    )
    imag_a = jnp.einsum("yabzl,abk->yzlk", parts[1], cos_a, precision=HIGH) - jnp.einsum(
        "yabzl,abk->yzlk", parts[0], sin_a, precision=HIGH
    )
    cos_t, sin_t = angle_table(index_inner[:, None], index_outer[None, :], length)
    real_t = real_a * cos_t + imag_a * sin_t
    imag_t = imag_a * cos_t - real_a * sin_t
    cos_b, sin_b = angle_table(index_inner[:, None], index_inner[None, :], inner)
    real_b = jnp.einsum("yzlk,lj->zyjk", real_t, cos_b, precision=HIGH) + jnp.einsum(
        "yzlk,lj->zyjk", imag_t, sin_b, precision=HIGH
    )
    imag_b = jnp.einsum("yzlk,lj->zyjk", imag_t, cos_b, precision=HIGH) - jnp.einsum(
        "yzlk,lj->zyjk", real_t, sin_b, precision=HIGH
    )
    real_b = real_b.reshape(levels, wave_rows, length) * scale
    imag_b = imag_b.reshape(levels, wave_rows, length) * scale
    return jnp.stack([real_b, imag_b])


def body(state, heights, surface_flag):
    levels = state.shape[1]
    level = lax.broadcasted_iota(jnp.int32, state.shape[1:], 0)
    fluid = (level >= heights[None]).astype(jnp.float32)
    surface = (level == heights[None]).astype(jnp.float32) * surface_flag[None].astype(jnp.float32)
    masked = state * fluid.astype(jnp.bfloat16)[None]
    padded = with_halo(masked, (("gx", 2), ("gy", 3)), 3).astype(jnp.float32)
    tendency = region_tendency(padded, fluid, surface)
    updated = masked[:2].astype(jnp.float32) + DT * tendency[:2].astype(jnp.float32)
    flows = with_halo(updated, (("gx", 2), ("gy", 3)), 1)
    vertical = masked[2].astype(jnp.float32) + DT * tendency[2].astype(jnp.float32)
    diverge = (
        flows[0, :, 2:, 1:-1]
        - flows[0, :, :-2, 1:-1]
        + (flows[1, :, 1:-1, 2:] - flows[1, :, 1:-1, :-2])
        + (raised(vertical) - lowered(vertical))
    ) * 0.5
    columns = lax.all_to_all(diverge, "gy", split_axis=1, concat_axis=2, tiled=True)
    total_y = columns.shape[2]
    spectrum_y = transform_y(columns)
    count_x = lax.axis_size("gx")
    count_y = lax.axis_size("gy")
    piece = total_y // (count_x * count_y)
    reordered = (
        spectrum_y.reshape(2, count_x, count_y, piece, -1)
        .transpose(0, 2, 1, 3, 4)
        .reshape(2, total_y, -1)
    )
    first = lax.all_to_all(reordered, "gy", split_axis=1, concat_axis=2, tiled=True)
    moved = lax.all_to_all(first, "gx", split_axis=1, concat_axis=2, tiled=True)
    order = (
        jnp.arange(count_x, dtype=jnp.int32)[:, None] * count_y
        + jnp.arange(count_y, dtype=jnp.int32)[None, :]
    )
    total_x = diverge.shape[1] * count_x
    scale = 1.0 / math.sqrt(total_x * total_y)
    spectrum = transform_x(moved, count_x, count_y, order, levels, scale)
    return (tendency, spectrum)


def solution(mesh):
    return jax.shard_map(
        body,
        mesh=mesh,
        in_specs=(P(None, None, "gx", "gy"), P("gx", "gy"), P("gx", "gy")),
        out_specs=(P(None, None, "gx", "gy"), P(None, None, ("gx", "gy"), None)),
        check_vma=False,
    )
```

profile of v0, /device:TPU:13, one launch (start us, length us, event | category | flops | bytes accessed | tf_op | source)
XLA Modules:
  0.0 766.3 jit_solution(2175216382204199542)
XLA Ops:
  2.7 10.9 %copy_multiply_fusion = bf16[4,2,256,2048]{3,0,2,1:T(4,128)(2,1)S(1)} fusion(bf16[4,2,256,2048]{3,2,1,0:T(8,128)(2,1)} %param.3, bf16[2,256,2048]{2,1,0:T(8,128)(2,1)S(1)} %convert_convert_fusion), kind=kLoop, calls=%fused_computation.4 | loop fusion | flops 4194304 | bytes 18874368 | tf_op jit(solution)/shard_map/mul | solution.py:154
  18.9 11.4 %copy.121 = bf16[4,2,256,2048]{3,2,1,0:T(8,128)(2,1)} copy(bf16[4,2,256,2048]{3,0,2,1:T(4,128)(2,1)} %copy-done.2) | data formatting | bytes 16777216 | tf_op jit(solution)/shard_map/mul | solution.py:154
  42.0 9.7 %slice_convert_fusion = f32[1,2,256,2048]{3,0,2,1:T(1,128)} fusion(bf16[4,2,256,2048]{3,0,2,1:T(4,128)(2,1)} %copy-done.2), kind=kLoop, calls=%fused_computation.56 | loop fusion | flops 1048576 | bytes 6291456 | tf_op jit(solution)/shard_map/convert_element_type | solution.py:159
  52.4 16.9 %concatenate.55 = bf16[4,2,262,2054]{3,2,1,0:T(8,128)(2,1)} concatenate(bf16[4,2,262,3]{3,2,1,0:T(8,128)(2,1)S(1)} %copy.125, bf16[4,2,262,2048]{3,2,1,0:T(8,128)(2,1)} %copy-done.4, bf16[4,2,262,3]{3,2,1,0:T(8,128)(2,1)S(1)} %copy.126), dimensions={3} | concatenate | bytes 17220736 | tf_op jit(solution)/shard_map/concatenate | solution.py:24
  69.3 11.1 %convert_element_type.115 = f32[4,2,262,2054]{3,2,1,0:T(8,128)} convert(bf16[4,2,262,2054]{3,2,1,0:T(8,128)(2,1)} %concatenate.55) | non-fusion elementwise | flops 4305184 | bytes 25831104 | tf_op jit(solution)/shard_map/convert_element_type | solution.py:155
  80.4 15.3 %slice_bitcast_fusion.14 = (f32[1,256,2048]{2,1,0:T(8,128)}, f32[1,256,2048]{2,1,0:T(8,128)}, f32[1,256,2048]{2,1,0:T(8,128)}, f32[1,256,2048]{2,1,0:T(8,128)}, ...) fusion(f32[4,2,262,2054]{3,2,1,0:T(8,128)} %convert_element_type.115), kind=kLoop, calls=%fused_computation.176 | loop fusion | bytes 33554432 | tf_op jit(solution)/shard_map/slice | solution.py:30
  97.9 6.9 slice_bitcast_fusion.3
  104.8 36.8 %fusion.118 = bf16[1,2,256,2048]{3,2,1,0:T(8,128)(2,1)} fusion(f32[4,2,262,2054]{3,2,1,0:T(8,128)} %convert_element_type.115, f32[2,262,2054]{2,1,0:T(8,128)} %get-tuple-element.23, f32[1,256,2048]{2,1,0:T(8,128)} %get-tuple-element.17, f32[1,256,2048]{2,1,0:T(8,128)} %get-tuple-element.18, s32[256,2048]{1,0:T(8,128)} %param.4), kind=kLoop, calls=%fused_computation.177 | loop fusion | flops 38797312 | bytes 71303168 | tf_op jit(solution)/shard_map/stack | solution.py:85
  141.7 21.6 %fusion.119 = bf16[1,2,256,2048]{3,2,1,0:T(8,128)(2,1)} fusion(f32[4,2,262,2054]{3,2,1,0:T(8,128)} %convert_element_type.115, f32[2,262,2054]{2,1,0:T(8,128)S(1)} %bitcast.196, f32[1,256,2048]{2,1,0:T(8,128)} %get-tuple-element.19, f32[1,256,2048]{2,1,0:T(8,128)} %get-tuple-element.12, s32[256,2048]{1,0:T(8,128)S(1)} %copy-done.3), kind=kLoop, calls=%fused_computation.178 | loop fusion | flops 38797312 | bytes 71303168 | tf_op jit(solution)/shard_map/stack | solution.py:85
  174.4 23.2 %bitcast_add_fusion = (f32[2,256,2048]{2,1,0:T(8,128)}, bf16[2,256,2048]{2,1,0:T(8,128)(2,1)}) fusion(f32[1,2,256,2048]{3,0,2,1:T(1,128)} %slice_convert_fusion, f32[4,2,262,2054]{3,2,1,0:T(8,128)} %convert_element_type.115, f32[2,262,2054]{2,1,0:T(8,128)S(1)} %bitcast.194, f32[1,256,2048]{2,1,0:T(8,128)} %get-tuple-element.15, ...), kind=kLoop, calls=%fused_computation.134 | loop fusion | flops 44040192 | bytes 83886080 | tf_op jit(solution)/shard_map/add | solution.py:159
  206.4 10.2 %fusion.42 = f32[2,256,2048]{2,1,0:T(8,128)S(1)} fusion(f32[2,2,258,1]{3,2,1,0:T(8,128)S(1)} %copy.137, f32[2,2,1,2048]{3,2,1,0:T(1,128)S(1)} %copy.129, f32[2,2,256,2048]{3,2,1,0:T(8,128)} %copy-done.1, f32[2,2,1,2048]{3,2,1,0:T(1,128)S(1)} %copy.131, f32[2,2,258,1]{3,2,1,0:T(8,128)S(1)} %copy.135, f32[1,256,2048]{2,1,0:T(8,128)} %get-tuple-element.39, ...), kind=kLoop, calls=%fused_computation.62 | loop fusion | flops 14680064 | bytes 16851008 | tf_op jit(solution)/shard_map/mul | solution.py:160
  227.6 46.9 %all-to-all-done = f32[2,256,2048]{2,0,1:T(2,128)} async-done(((f32[2,256,2048]{2,0,1:T(2,128)}), f32[2,256,2048]{2,0,1:T(2,128)}, u32[]{:S(2)}, u32[]{:S(2)}) %all-to-all-start) | async-done | bytes 4194336 | tf_op jit(solution)/shard_map/all_to_all | solution.py:166
  274.5 9.2 %copy.139 = f32[2,2,128,2048]{2,0,3,1:T(2,128)} copy(f32[2,2,128,2048]{3,0,2,1:T(2,128)} %bitcast.26) | data formatting | bytes 8388608 | tf_op jit(solution)/shard_map/all_to_all | solution.py:166
  283.7 6.4 reshape.173
  290.1 9.0 %fusion.104 = f32[64,256,64]{1,0,2:T(8,128)S(1)} fusion(f32[256,64,64]{0,2,1:T(8,128)} %reshape.173), kind=kOutput, calls=%fused_computation.163 | convolution fusion | flops 805363712 | bytes 8388608 | tf_op jit(solution)/shard_map/mpl,pk->klm/dot_general | solution.py:103
  299.1 8.1 %add_bitcast_fusion = (f32[64,64,256]{2,0,1:T(8,128)S(1)}, f32[64,64,256]{2,0,1:T(8,128)S(1)}) fusion(f32[64,256,64]{1,0,2:T(8,128)S(1)} %fusion.104, f32[64,64]{0,1:T(8,128)S(1)} %get-tuple-element.40, f32[64,64]{0,1:T(8,128)S(1)} %get-tuple-element.41, f32[256,64,64]{0,2,1:T(8,128)S(1)} %copy-done.7), kind=kOutput, calls=%fused_computation.143 | convolution fusion | flops 812703744 | bytes 16809984 | tf_op jit(solution)/shard_map/mpl,pk->klm/dot_general | solution.py:102
  307.2 6.5 fusion.96
  313.7 6.3 fusion.98
  320.1 6.7 fusion.108
  326.7 6.4 fusion.111
  340.0 20.8 %copy.149 = f32[2,4096,256]{2,0,1:T(2,128)S(1)} copy(f32[2,4096,256]{2,1,0:T(8,128)S(1)} %bitcast.198) | data formatting | bytes 16777216 | tf_op jit(solution)/shard_map/reshape | solution.py:175
  360.8 95.3 %all_to_all.48 = f32[2,4096,256]{2,0,1:T(2,128)S(1)} all-to-all(f32[2,4096,256]{2,0,1:T(2,128)S(1)} %copy.149), channel_id=1, replica_groups=mesh['gx'=16,'gy'=2] {'gy'}, dimensions={1} | all-to-all | bytes 16777216 | tf_op jit(solution)/shard_map/all_to_all | solution.py:177
  460.1 8.7 %copy.151 = f32[2,2048,2,256]{1,3,2,0:T(8,128)} copy(f32[2,2048,2,256]{3,1,2,0:T(8,128)} %bitcast.199) | data formatting | bytes 16777216 | tf_op jit(solution)/shard_map/all_to_all | solution.py:177
  468.8 13.1 %copy.152 = f32[2,2048,512]{2,0,1:T(2,128)} copy(f32[2,2048,512]{1,2,0:T(8,128)} %bitcast.200) | data formatting | bytes 16777216 | tf_op jit(solution)/shard_map/all_to_all | solution.py:177
  481.9 7.2 all-to-all-start.2
  492.6 36.6 %fusion.120 = bf16[1,2,256,2048]{3,2,1,0:T(8,128)(2,1)} fusion(f32[256,2048]{1,0:T(8,128)} %convert_element_type.119, f32[4,2,262,2054]{3,2,1,0:T(8,128)} %convert_element_type.115, f32[2,262,2054]{2,1,0:T(8,128)} %get-tuple-element.21, f32[1,256,2048]{2,1,0:T(8,128)S(1)} %copy-done.10, f32[1,256,2048]{2,1,0:T(8,128)} %get-tuple-element.14, ...), kind=kLoop, calls=%fused_computation.179 | loop fusion | flops 41943040 | bytes 77594624 | tf_op jit(solution)/shard_map/stack | solution.py:85
  535.3 136.0 %all-to-all-done.2 = f32[2,2048,512]{2,0,1:T(2,128)} async-done(((f32[2,2048,512]{2,0,1:T(2,128)}), f32[2,2048,512]{2,0,1:T(2,128)}, u32[]{:S(2)}, u32[]{:S(2)}) %all-to-all-start.2) | async-done | bytes 8388640 | tf_op jit(solution)/shard_map/all_to_all | solution.py:178
  702.4 6.3 fusion.162
  728.5 6.5 fusion.90
  735.0 6.4 multiply_bitcast_fusion.1
  741.3 6.9 multiply_bitcast_fusion
  757.0 8.9 %copy.166 = f32[2,2,128,4096]{3,2,1,0:T(8,128)} copy(f32[2,2,128,4096]{2,3,1,0:T(8,128)} %pad_maximum_fusion.2) | data formatting | bytes 16777216
  (96 shorter events, 132.5 us)
Async XLA Ops:
  13.6 3.4 copy-start.2
  17.1 13.3 %collective-permute-start = (bf16[4,2,3,2048]{3,0,2,1:T(4,128)(2,1)S(1)}, bf16[4,2,3,2048]{3,0,2,1:T(4,128)(2,1)S(1)}, u32[]{:S(2)}, u32[]{:S(2)}) collective-permute-start(bf16[4,2,3,2048]{3,0,2,1:T(4,128)(2,1)S(1)} %get-tuple-element.36), channel_id=1, source_target_pairs={{0,2},{2,4},{4,6},{6,8},{8,10},{10,12},{12,14},{14,16},{16,18},{18... | collective-permute-start | bytes 294920 | tf_op jit(solution)/shard_map/ppermute | solution.py:22
  18.9 11.5 %collective-permute-start.1 = (bf16[4,2,3,2048]{3,0,2,1:T(4,128)(2,1)S(1)}, bf16[4,2,3,2048]{3,0,2,1:T(4,128)(2,1)S(1)}, u32[]{:S(2)}, u32[]{:S(2)}) collective-permute-start(bf16[4,2,3,2048]{3,0,2,1:T(4,128)(2,1)S(1)} %get-tuple-element.37), channel_id=1, source_target_pairs={{2,0},{4,2},{6,4},{8,6},{10,8},{12,10},{14,12},{16,14},{18,16},{20... | collective-permute-start | bytes 294920 | tf_op jit(solution)/shard_map/ppermute | solution.py:23
  36.2 3.4 copy-start.4
  40.5 11.5 %collective-permute-start.2 = (bf16[4,2,262,3]{2,0,3,1:T(4,128)(2,1)S(1)}, bf16[4,2,262,3]{2,0,3,1:T(4,128)(2,1)S(1)}, u32[]{:S(2)}, u32[]{:S(2)}) collective-permute-start(bf16[4,2,262,3]{2,0,3,1:T(4,128)(2,1)S(1)} %copy.123), channel_id=1, source_target_pairs={{0,1},{1,0},{2,3},{3,2},{4,5},{5,4},{6,7},{7,6},{8,9},{9,8},{10,11... | collective-permute-start | bytes 37736 | tf_op jit(solution)/shard_map/ppermute | solution.py:22
  41.7 9.9 %collective-permute-start.3 = (bf16[4,2,262,3]{2,0,3,1:T(4,128)(2,1)S(1)}, bf16[4,2,262,3]{2,0,3,1:T(4,128)(2,1)S(1)}, u32[]{:S(2)}, u32[]{:S(2)}) collective-permute-start(bf16[4,2,262,3]{2,0,3,1:T(4,128)(2,1)S(1)} %copy.124), channel_id=1, source_target_pairs={{1,0},{0,1},{3,2},{2,3},{5,4},{4,5},{7,6},{6,7},{9,8},{8,9},{11,10... | collective-permute-start | bytes 37736 | tf_op jit(solution)/shard_map/ppermute | solution.py:23
  80.4 17.5 %copy-start = (f32[4,2,262,2054]{3,2,1,0:T(8,128)S(1)}, f32[4,2,262,2054]{3,2,1,0:T(8,128)}, u32[]{:S(2)}) copy-start(f32[4,2,262,2054]{3,2,1,0:T(8,128)} %convert_element_type.115) | copy-start | bytes 51662212
  104.8 36.8 %slice-start.2 = ((s8[4595712]{0:T(1024)(128)(4,1)}), s8[4194304]{0:T(1024)(128)(4,1)S(1)}, s32[]{:S(2)}) async-start(s8[4595712]{0:T(1024)(128)(4,1)} %bitcast.195), calls=%async_computation.5 | async-start | bytes 8388608
  104.8 36.8 %slice-start.3 = ((s8[4595712]{0:T(1024)(128)(4,1)}), s8[401408]{0:T(1024)(128)(4,1)S(1)}, s32[]{:S(2)}) async-start(s8[4595712]{0:T(1024)(128)(4,1)} %bitcast.195), calls=%async_computation.6 | async-start | bytes 802816
  104.8 36.8 %copy-start.3 = (s32[256,2048]{1,0:T(8,128)S(1)}, s32[256,2048]{1,0:T(8,128)}, u32[]{:S(2)}) copy-start(s32[256,2048]{1,0:T(8,128)} %param.4) | copy-start | bytes 6291460
  141.7 32.7 %slice-start = ((s8[4595712]{0:T(1024)(128)(4,1)}), s8[4194304]{0:T(1024)(128)(4,1)S(1)}, s32[]{:S(2)}) async-start(s8[4595712]{0:T(1024)(128)(4,1)} %bitcast.193), calls=%async_computation.3 | async-start | bytes 8388608
  141.7 32.7 %slice-start.1 = ((s8[4595712]{0:T(1024)(128)(4,1)}), s8[401408]{0:T(1024)(128)(4,1)S(1)}, s32[]{:S(2)}) async-start(s8[4595712]{0:T(1024)(128)(4,1)} %bitcast.193), calls=%async_computation.4 | async-start | bytes 802816
  167.5 3.4 copy-start.1
  171.0 26.5 %collective-permute-start.4 = (f32[2,2,1,2048]{3,1,2,0:T(2,128)S(1)}, f32[2,2,1,2048]{3,1,2,0:T(2,128)S(1)}, u32[]{:S(2)}, u32[]{:S(2)}) collective-permute-start(f32[2,2,1,2048]{3,1,2,0:T(2,128)S(1)} %copy.128), channel_id=1, source_target_pairs={{2,0},{4,2},{6,4},{8,6},{10,8},{12,10},{14,12},{16,14},{18,16},{20... | collective-permute-start | bytes 98312 | tf_op jit(solution)/shard_map/ppermute | solution.py:23
  172.3 25.3 %collective-permute-start.5 = (f32[2,2,1,2048]{3,1,2,0:T(2,128)S(1)}, f32[2,2,1,2048]{3,1,2,0:T(2,128)S(1)}, u32[]{:S(2)}, u32[]{:S(2)}) collective-permute-start(f32[2,2,1,2048]{3,1,2,0:T(2,128)S(1)} %copy.130), channel_id=1, source_target_pairs={{0,2},{2,4},{4,6},{6,8},{8,10},{10,12},{12,14},{14,16},{16,18},{18... | collective-permute-start | bytes 98312 | tf_op jit(solution)/shard_map/ppermute | solution.py:22
  199.7 6.4 collective-permute-start.7
  200.9 5.0 collective-permute-start.6
  221.8 52.7 %all-to-all-start = ((f32[2,256,2048]{2,0,1:T(2,128)}), f32[2,256,2048]{2,0,1:T(2,128)}, u32[]{:S(2)}, u32[]{:S(2)}) async-start(f32[2,256,2048]{2,0,1:T(2,128)} %copy.138), calls=%async_computation | async-start | bytes 8388608 | tf_op jit(solution)/shard_map/all_to_all | solution.py:166
  290.1 9.0 %copy-start.7 = (f32[256,64,64]{0,2,1:T(8,128)S(1)}, f32[256,64,64]{0,2,1:T(8,128)}, u32[]{:S(2)}) copy-start(f32[256,64,64]{0,2,1:T(8,128)} %reshape.173) | copy-start | bytes 12582916
  481.9 189.4 %all-to-all-start.2 = ((f32[2,2048,512]{2,0,1:T(2,128)}), f32[2,2048,512]{2,0,1:T(2,128)}, u32[]{:S(2)}, u32[]{:S(2)}) async-start(f32[2,2048,512]{2,0,1:T(2,128)} %copy.152), calls=%async_computation.2 | async-start | bytes 16777216 | tf_op jit(solution)/shard_map/all_to_all | solution.py:178
  489.1 3.4 copy-start.10
  492.6 36.6 %copy-start.8 = (bf16[1,2,256,2048]{3,2,1,0:T(8,128)(2,1)S(1)}, bf16[1,2,256,2048]{3,2,1,0:T(8,128)(2,1)}, u32[]{:S(2)}) copy-start(bf16[1,2,256,2048]{3,2,1,0:T(8,128)(2,1)} %fusion.118) | copy-start | bytes 6291460
  492.6 36.6 %copy-start.9 = (bf16[1,2,256,2048]{3,2,1,0:T(8,128)(2,1)S(1)}, bf16[1,2,256,2048]{3,2,1,0:T(8,128)(2,1)}, u32[]{:S(2)}) copy-start(bf16[1,2,256,2048]{3,2,1,0:T(8,128)(2,1)} %fusion.119) | copy-start | bytes 6291460
  702.4 6.3 copy-start.6
  708.7 3.9 copy-start.5
where the time goes:
time: 774 us; the launch traced here: 766 us
  local copies, waits for them, and re-layouts  189 us (24%)
  other arithmetic  188 us (24%)
  waiting for transfers between devices  183 us (24%)
  blocking collectives  95.3 us (12%)
  matrix products  88.7 us (11%)
  starting transfers between devices  21 us (3%)
    all_to_all x1, waiting for transfers between devices, body(): moved = lax.all_to_all(first, 'gx', split_axis=1, concat_axis=2, tiled=True)  136 us
    another operation x4, other arithmetic, region_tendency(): return jnp.stack(pieces)  101 us
    all_to_all x1, blocking collectives, body(): lax.all_to_all(reordered, 'gy', split_axis=1, concat_axis=2, tiled=True)  95.3 us
    all_to_all x1, waiting for transfers between devices, body(): lax.all_to_all(diverge, 'gy', split_axis=1, concat_axis=2, tiled=True)  46.9 us
    all_to_all x3, local copies, waits for them, and re-layouts, body(): lax.all_to_all(reordered, 'gy', split_axis=1, concat_axis=2, tiled=True)  25.8 us
    add x1, other arithmetic, body(): masked[2].astype(jnp.float32) + DT * tendency[2].astype(jnp.float32)  23.2 us
    unnamed x31, local copies, waits for them, and re-layouts  21.3 us
    reshape x1, local copies, waits for them, and re-layouts, body(): reordered = spectrum_y.reshape(2, count_x, count_y, piece, -1).transpose(...  20.8 us
  transfers between devices with their start and end apart: 10, of which 2 were waited for; matrix products, arithmetic and copies ran while one was open for 13% of the time, Pallas kernels for 0%

commit v1 on v0

v1 whole, which is shorter than its diff:
```python
import functools
import math

import jax
import jax.numpy as jnp
import numpy as np
from jax import lax
from jax.experimental import pallas as pl
from jax.experimental.pallas import tpu as pltpu
from jax.sharding import PartitionSpec as P

NU = 0.1
BETA = 0.5
HEAT = 1.0
DT = 0.5
RADIX = 16
SEND = jnp.float16
BF = jnp.bfloat16
F32 = jnp.float32
SLOPE = {1: 45.0, -1: -45.0, 2: -9.0, -2: 9.0, 3: 1.0, -3: -1.0}
CURVE_X = {1: 1.0, -1: 1.0}
CURVE_Y = {0: -6.0, 1: 1.0, -1: 1.0}
CENTRAL = {1: 1.0, -1: -1.0}


def band(rows, columns, offset, taps):
    step = np.arange(rows)[:, None] - np.arange(columns)[None, :] - offset
    out = np.zeros((rows, columns), np.float32)
    for key, value in taps.items():
        out[step == key] = value
    return out


def dot(a, b):
    return jnp.dot(a, b, preferred_element_type=F32)


def dot_t(a, b):
    return lax.dot_general(a, b, (((1,), (1,)), ((), ())), preferred_element_type=F32)


def stencil_kernel(
    bx, width,
    main, prev, nxt, heights, h_prev, h_next, flag, xlo, xhi, yl, yr, dy, dx, sy, sx,
    tend, div0, div1,
    m_s, h_s, t_s,
):
    i = pl.program_id(0)
    last = pl.num_programs(0) - 1
    rows = bx + 16
    ext = width + 256
    mine = slice(8, 8 + bx)
    divs = (div0, div1)
    side = pl.ds(pl.multiple_of(i * bx, 16), rows)


    piece = 256

    def fill(c, carry):
        lanes = pl.ds(pl.multiple_of(c * piece, 128), piece)
        target = pl.ds(pl.multiple_of(128 + c * piece, 128), piece)

        def edge(field, ref_low, ref_high, middle):
            low = jnp.where(i == 0, xlo[field, :, lanes].astype(F32), ref_low)
            high = jnp.where(i == last, xhi[field, :, lanes].astype(F32), ref_high)
            return jnp.concatenate([low, middle, high], axis=0)

        h = edge(
            8, h_prev[:, lanes].astype(F32), h_next[:, lanes].astype(F32),
            heights[:, lanes].astype(F32),
        )
        h_s[:, target] = h
        for f in range(8):
            value = edge(
                f, prev[f // 2, f % 2, :, lanes].astype(F32)[8:],
                nxt[f // 2, f % 2, :, lanes].astype(F32)[:8],
                main[f // 2, f % 2, :, lanes].astype(F32),
            )
            m_s[f, :, target] = jnp.where(h <= float(f % 2), value, 0.0).astype(BF)
        return carry

    lax.fori_loop(0, width // piece, fill, 0)
    for ref, target in ((yl, slice(0, 128)), (yr, slice(width + 128, ext))):
        h = ref[8, side, :].astype(F32)
        h_s[:, target] = h
        for f in range(8):
            m_s[f, :, target] = jnp.where(
                h <= float(f % 2), ref[f, side, :].astype(F32), 0.0
            ).astype(BF)

    def tendency(f, lanes, window, matrix, centers, fluids, n):
        k = f % 2
        mid = m_s[f, :, lanes]
        along_y = dot(m_s[f, :, window], matrix)
        along_x = dot(dx[...], mid)
        other = m_s[f + 1 - 2 * k, :, lanes].astype(F32)
        u60, v60, wz = centers[k]
        lap = along_y[:, n:] + along_x[rows:] + other
        out = NU * lap - (u60 * along_x[:rows] + v60 * along_y[:, :n] + wz * other)
        return out

    def centers_of(lanes):
        out = []
        for k in range(2):
            sign = 0.5 if k == 0 else -0.5
            out.append((
                m_s[k, :, lanes].astype(F32) * (1.0 / 60.0),
                m_s[2 + k, :, lanes].astype(F32) * (1.0 / 60.0),
                m_s[4 + k, :, lanes].astype(F32) * sign,
            ))
        return out

    def first(j, carry):
        start = pl.multiple_of(j * 256, 128)
        lanes = pl.ds(pl.multiple_of(start + 128, 128), 256)
        window = pl.ds(start, 512)
        outs = pl.ds(start, 256)
        centers = centers_of(lanes)
        h = h_s[:, lanes]
        fluids = [(h <= float(k)).astype(F32) for k in range(2)]
        shine = flag[:, outs].astype(F32)
        stars = []
        for k in range(2):
            for c in (0, 1, 2, 3):
                f = 2 * c + k
                t = tendency(f, lanes, window, dy[...], centers, fluids, 256)
                if c == 2:
                    t = t + BETA * m_s[6 + k, :, lanes].astype(F32)
                if c == 3:
                    t = t[mine] + HEAT * jnp.where(h[mine] == float(k), shine, 0.0)
                    tend[c, k, :, outs] = (fluids[k][mine] * t).astype(BF)
                    continue
                t = fluids[k] * t
                tend[c, k, :, outs] = t[mine].astype(BF)
                if c == 0:
                    tb = t.astype(BF)
                    divs[k][:, outs] = dot(sx[0], m_s[f, :, lanes]) + dot(sx[1], tb)
                if c == 1:
                    t_s[k, :, lanes] = t.astype(BF)
                if c == 2:
                    tb = t[mine].astype(BF).astype(F32)
                    stars.append(m_s[f, :, lanes].astype(F32)[mine] + DT * tb)
        div0[:, outs] += stars[1]
        div1[:, outs] -= stars[0]
        return carry

    lax.fori_loop(0, width // 256, first, 0)

    for target, window, matrix in (
        (slice(0, 128), slice(0, 256),
         jnp.concatenate([dy[128:384, 0:128], dy[128:384, 256:384]], axis=1)),
        (slice(ext - 128, ext), slice(ext - 256, ext),
         jnp.concatenate([dy[0:256, 0:128], dy[0:256, 256:384]], axis=1)),
    ):
        centers = centers_of(target)
        h = h_s[:, target]
        for k in range(2):
            t = tendency(2 + k, target, window, matrix, centers, None, 128)
            t_s[k, :, target] = jnp.where(h <= float(k), t, 0.0).astype(BF)

    def second(j, carry):
        start = pl.multiple_of(j * 256, 128)
        window = pl.ds(start, 512)
        outs = pl.ds(start, 256)
        for k in range(2):
            part = dot(m_s[2 + k, :, window], sy[0]) + dot(t_s[k, :, window], sy[1])
            divs[k][:, outs] = (divs[k][:, outs] + part[mine]) * 0.5
        return carry

    lax.fori_loop(0, width // 256, second, 0)


def stencil(state, heights, flag, xlo, xhi, yl, yr):
    _, _, length, width = state.shape
    bx = min(128, length)
    rows = bx + 16
    ext = width + 256
    dy = np.concatenate([band(512, 256, 128, SLOPE), band(512, 256, 128, CURVE_Y)], axis=1)
    dx = np.concatenate([band(rows, rows, 0, SLOPE).T, band(rows, rows, 0, CURVE_X).T], axis=0)
    sy = band(512, 256, 128, CENTRAL)
    sy = np.stack([sy, DT * sy])
    sx = band(rows, bx, 8, CENTRAL).T
    sx = np.stack([sx, DT * sx])
    n16 = length // 16
    n8 = length // 8
    full = lambda *shape: pl.BlockSpec(shape, lambda i: (0,) * len(shape))
    return pl.pallas_call(
        functools.partial(stencil_kernel, bx, width),
        grid=(length // bx,),
        out_shape=(
            jax.ShapeDtypeStruct(state.shape, BF),
            jax.ShapeDtypeStruct((length, width), F32),
            jax.ShapeDtypeStruct((length, width), F32),
        ),
        in_specs=[
            pl.BlockSpec((4, 2, bx, width), lambda i: (0, 0, i, 0)),
            pl.BlockSpec((4, 2, 16, width), lambda i: (0, 0, jnp.maximum(i * (bx // 16) - 1, 0), 0)),
            pl.BlockSpec((4, 2, 16, width), lambda i: (0, 0, jnp.minimum((i + 1) * (bx // 16), n16 - 1), 0)),
            pl.BlockSpec((bx, width), lambda i: (i, 0)),
            pl.BlockSpec((8, width), lambda i: (jnp.maximum(i * (bx // 8) - 1, 0), 0)),
            pl.BlockSpec((8, width), lambda i: (jnp.minimum((i + 1) * (bx // 8), n8 - 1), 0)),
            pl.BlockSpec((bx, width), lambda i: (i, 0)),
            full(9, 8, width),
            full(9, 8, width),
            full(9, length + 16, 128),
            full(9, length + 16, 128),
            full(512, 512),
            full(2 * rows, rows),
            full(2, 512, 256),
            full(2, bx, rows),
        ],
        out_specs=(
            pl.BlockSpec((4, 2, bx, width), lambda i: (0, 0, i, 0)),
            pl.BlockSpec((bx, width), lambda i: (i, 0)),
            pl.BlockSpec((bx, width), lambda i: (i, 0)),
        ),
        scratch_shapes=[
            pltpu.VMEM((8, rows, ext), BF),
            pltpu.VMEM((rows, ext), F32),
            pltpu.VMEM((2, rows, ext), BF),
        ],
        compiler_params=pltpu.CompilerParams(vmem_limit_bytes=56 * 2**20),
        name="stencil",
    )(state, state, state, heights, heights, heights, flag, xlo, xhi, yl, yr,
      jnp.asarray(dy, BF), jnp.asarray(dx, BF), jnp.asarray(sy, BF), jnp.asarray(sx, BF))


def fft(values):
    n = len(values)
    if n == 1:
        return values
    even, odd = fft(values[0::2]), fft(values[1::2])
    out = [None] * n
    for k in range(n // 2):
        er, ei = even[k]
        pr, pi = rotate(odd[k], k, n)
        out[k] = (er + pr, ei + pi)
        out[k + n // 2] = (er - pr, ei - pi)
    return out


def rotate(value, k, n):
    re, im = value
    if k == 0:
        return re, im
    if 4 * k == n:
        return im, -re
    if 8 * k == n:
        root = math.sqrt(0.5)
        return (re + im) * root, (im - re) * root
    if 8 * k == 3 * n:
        root = math.sqrt(0.5)
        return (im - re) * root, -(re + im) * root
    c, s = math.cos(2 * math.pi * k / n), math.sin(2 * math.pi * k / n)
    return re * c + im * s, im * c - re * s


def rfft(values):
    n = len(values)
    if n == 2:
        a, b = values
        return [(a + b, None), (a - b, None)]
    even, odd = rfft(values[0::2]), rfft(values[1::2])
    half = n // 2

    def at(part, k):
        if k <= half // 2:
            return part[k]
        re, im = part[half - k]
        return re, None if im is None else -im

    out = []
    for k in range(half + 1):
        er, ei = at(even, k % half)
        orr, oi = at(odd, k % half)
        if k == half:
            out.append((er - orr, None))
        elif k == 0:
            out.append((er + orr, None))
        elif 4 * k == n:
            out.append((er, -orr))
        else:
            if oi is None:
                c, s = math.cos(2 * math.pi * k / n), math.sin(2 * math.pi * k / n)
                pr, pi = orr * c, -orr * s
            else:
                pr, pi = rotate((orr, oi), k, n)
            out.append((er + pr, pi if ei is None else ei + pi))
    return out


def split(value):
    high = value.astype(BF)
    return high, (value - high.astype(F32)).astype(BF)


def complex_matrix(angle, scale):
    c, s = np.cos(angle) * scale, np.sin(angle) * scale
    full = np.block([[c, s], [-s, c]])
    high = full.astype(np.float32).astype(jnp.bfloat16)
    low = (full - high.astype(np.float64)).astype(jnp.bfloat16)
    return np.stack([high, low])


def y_kernel(inner, groups, each, f, tw, w, out, hi, lo):
    sources, length, width = f.shape
    chunks = width // inner

    def strip(i, carry):
        r = pl.ds(pl.multiple_of(i * 16, 16), 16)
        for c in range(inner // 128):
            lane = slice(c * 128, c * 128 + 128)
            values = []
            for q in range(RADIX):
                s, o = q // chunks, (q % chunks) * inner + c * 128
                values.append(f[s, r, o : o + 128].astype(F32))
            spec = rfft(values)
            for t in range(RADIX):
                re, im = spec[t if t <= RADIX // 2 else RADIX - t]
                cos = tw[0, t : t + 1, lane]
                sin = tw[1, t : t + 1, lane]
                if im is None:
                    zr, zi = re * cos, -(re * sin)
                elif t <= RADIX // 2:
                    zr, zi = re * cos + im * sin, im * cos - re * sin
                else:
                    zr, zi = re * cos - im * sin, -(im * cos + re * sin)
                zrh, zrl = split(zr)
                zih, zil = split(zi)
                hi[t, r, lane] = zrh
                lo[t, r, lane] = zrl
                lane_i = slice(inner + c * 128, inner + c * 128 + 128)
                hi[t, r, lane_i] = zih
                lo[t, r, lane_i] = zil
        return carry

    lax.fori_loop(0, length // 16, strip, 0)

    def multiply(t, carry):
        h = hi[t]
        got = dot_t(w[0], h) + dot_t(w[0], lo[t]) + dot_t(w[1], h)
        for part in range(2):
            for g in range(groups):
                base = (part * groups + g) * each
                for c in range(length // 128):
                    out[g, part, c, pl.ds(t, each, stride=RADIX), :] = got[
                        base : base + each, c * 128 : c * 128 + 128
                    ]
        return carry

    lax.fori_loop(0, RADIX, multiply, 0)


def transform_y(f, twiddle, matrix, groups, each):
    sources, length, width = f.shape
    inner = sources * width // RADIX
    return pl.pallas_call(
        functools.partial(y_kernel, inner, groups, each),
        out_shape=jax.ShapeDtypeStruct((groups, 2, length // 128, each * RADIX, 128), F32),
        in_specs=[pl.BlockSpec(memory_space=pltpu.VMEM)] * 3,
        out_specs=pl.BlockSpec(memory_space=pltpu.VMEM),
        scratch_shapes=[
            pltpu.VMEM((RADIX, length, 2 * inner), BF),
            pltpu.VMEM((RADIX, length, 2 * inner), BF),
        ],
        compiler_params=pltpu.CompilerParams(vmem_limit_bytes=56 * 2**20),
        cost_estimate=pl.CostEstimate(flops=10**10, bytes_accessed=10**7, transcendentals=0),
        name="transform_y",
    )(f, twiddle, matrix)


def x_kernel(z, tw, v, out, hi, lo, wide):
    count, _, pieces, waves, lanes_each = z.shape
    length = pieces * lanes_each
    inner = wide.shape[1] // count

    def strip(i, carry):
        r = pl.ds(pl.multiple_of(i * 16, 16), 16)
        for c in range(pieces):
            lane = slice(c * lanes_each, (c + 1) * lanes_each)
            values = [(z[a, 0, c, r, :].astype(F32), z[a, 1, c, r, :].astype(F32)) for a in range(count)]
            for t, (re, im) in enumerate(fft(values)):
                cos = tw[0, t : t + 1, lane]
                sin = tw[1, t : t + 1, lane]
                zrh, zrl = split(re * cos + im * sin)
                zih, zil = split(im * cos - re * sin)
                hi[t, r, lane] = zrh
                lo[t, r, lane] = zrl
                lane_i = slice(length + c * lanes_each, length + (c + 1) * lanes_each)
                hi[t, r, lane_i] = zih
                lo[t, r, lane_i] = zil
        return carry

    lax.fori_loop(0, waves // 16, strip, 0)

    def multiply(t, carry):
        h = hi[t]
        got = dot_t(v[0], h) + dot_t(v[0], lo[t]) + dot_t(v[1], h)
        for part in range(2):
            wide[part, pl.ds(t, inner, stride=count), :] = got[part * inner : (part + 1) * inner]
        return carry

    lax.fori_loop(0, count, multiply, 0)

    def turn(c, carry):
        block = pl.ds(pl.multiple_of(c * 256, 256), 256)
        for part in range(2):
            out[part, :, block] = wide[part, block, :].T[: out.shape[1]]
        return carry

    lax.fori_loop(0, wide.shape[1] // 256, turn, 0)


def transform_x(z, twiddle, matrix):
    count, _, pieces, waves, lanes_each = z.shape
    length = pieces * lanes_each
    total = count * length
    padded = max(waves, 128)
    return pl.pallas_call(
        x_kernel,
        out_shape=jax.ShapeDtypeStruct((2, waves, total), F32),
        in_specs=[pl.BlockSpec(memory_space=pltpu.VMEM)] * 3,
        out_specs=pl.BlockSpec(memory_space=pltpu.VMEM),
        scratch_shapes=[
            pltpu.VMEM((count, padded, 2 * length), BF),
            pltpu.VMEM((count, padded, 2 * length), BF),
            pltpu.VMEM((2, total, padded), F32),
        ],
        compiler_params=pltpu.CompilerParams(vmem_limit_bytes=56 * 2**20),
        cost_estimate=pl.CostEstimate(flops=10**10, bytes_accessed=10**7, transcendentals=0),
        name="transform_x",
    )(z, twiddle, matrix)


def tables(count_x, count_y, length, width):
    total_x, total_y = count_x * length, count_y * width
    inner = total_y // RADIX
    waves = total_y // (count_x * count_y)
    each = waves // RADIX
    p = np.arange(inner)
    shift = np.arange(RADIX)[None, :, None] + waves * np.arange(count_y)[:, None, None]
    angle = 2 * np.pi * ((shift * p) % total_y) / total_y
    tw_y = np.stack([np.cos(angle), np.sin(angle)], axis=1).astype(np.float32)
    m = ((np.arange(count_x) * count_y * each)[:, None] + np.arange(each)[None, :]).reshape(-1)
    w = complex_matrix(2 * np.pi * ((m[:, None] * p[None, :]) % inner) / inner, 1 / math.sqrt(total_y))
    l = np.arange(length)
    angle = 2 * np.pi * ((np.arange(count_x)[:, None] * l[None, :]) % total_x) / total_x
    tw_x = np.stack([np.cos(angle), np.sin(angle)]).astype(np.float32)
    v = complex_matrix(2 * np.pi * ((l[:, None] * l[None, :]) % length) / length, 1 / math.sqrt(total_x))
    return tw_y, w, tw_x, v, each


def around(axis, first, final):
    count = lax.axis_size(axis)
    up = [(i, (i + 1) % count) for i in range(count)]
    down = [(j, i) for i, j in up]
    return lax.ppermute(final, axis, up), lax.ppermute(first, axis, down)


def body(state, heights, flag):
    _, levels, length, width = state.shape
    count_x, count_y = lax.axis_size("gx"), lax.axis_size("gy")
    tw_y, w, tw_x, v, each = tables(count_x, count_y, length, width)

    def pieces(lo, hi, axis):
        s = lax.slice_in_dim(state, lo, hi, axis=axis + 2)
        s = s.reshape((8,) + s.shape[2:])
        return jnp.concatenate([s, lax.slice_in_dim(heights, lo, hi, axis=axis)[None].astype(BF)], axis=0)

    xlo, xhi = around("gx", pieces(0, 8, 0), pieces(length - 8, length, 0))
    left = jnp.concatenate([xlo[:, :, :4], pieces(0, 4, 1), xhi[:, :, :4]], axis=1)
    right = jnp.concatenate(
        [xlo[:, :, width - 4 :], pieces(width - 4, width, 1), xhi[:, :, width - 4 :]], axis=1
    )
    before, after = around("gy", left, right)
    yl = jnp.pad(before, ((0, 0), (0, 0), (124, 0)))
    yr = jnp.pad(after, ((0, 0), (0, 0), (0, 124)))
    tendency, div0, div1 = stencil(state, heights, flag, xlo, xhi, yl, yr)

    mine = lax.axis_index("gy")
    twiddle = lax.dynamic_index_in_dim(jnp.asarray(tw_y), mine, 0, keepdims=False)
    results = []
    for div in (div0, div1):
        lines = lax.all_gather(div.astype(SEND), "gy", axis=0).astype(F32)
        waves = transform_y(lines, twiddle, jnp.asarray(w), count_x, each)
        moved = lax.all_to_all(waves.astype(SEND), "gx", split_axis=0, concat_axis=0, tiled=True)
        results.append(transform_x(moved.astype(F32), jnp.asarray(tw_x), jnp.asarray(v)))
    return tendency, jnp.stack(results, axis=1)


def solution(mesh):
    return jax.shard_map(
        body,
        mesh=mesh,
        in_specs=(P(None, None, "gx", "gy"), P("gx", "gy"), P("gx", "gy")),
        out_specs=(P(None, None, "gx", "gy"), P(None, None, ("gx", "gy"), None)),
        check_vma=False,
    )
```

time: 774 us -> 254 us (0.33)
  local copies, waits for them, and re-layouts: 189 us -> 11.4 us
  other arithmetic: 188 us -> 27.5 us
  waiting for transfers between devices: 183 us -> 33.1 us
  Pallas kernels: 0 us -> 112 us
  matrix products: 88.7 us -> 0 us
  blocking collectives: 95.3 us -> 47.6 us
    all_to_all x2, waiting for transfers between devices: 183 us -> 26.7 us  [body(): lax.all_to_all(waves.astype(SEND), 'gx', split_axis=0, concat_axis=0, til...]
    pallas_call x0 -> x5, Pallas kernels: none -> 112 us  [the longest x1 44.1 us: stencil(): pl.pallas_call(functools.partial(stencil_kernel, bx, width), grid=(length...]
    another operation x5 -> x2, other arithmetic: 105 us -> 4.5 us  [the longest x1 2.73 us: body(): return (tendency, jnp.stack(results, axis=1))]
    all_to_all x1 -> x0, blocking collectives: 95.3 us -> none  [body(): lax.all_to_all(reordered, 'gy', split_axis=1, concat_axis=2, tiled=True)]
    dot_general x14 -> x0, matrix products: 88.7 us -> none  [the longest x1 8.98 us: transform_y(): imag_a = -jnp.einsum('mpl,pk->klm', flat, sin_a, precision=HIGH)]
    all_gather x0 -> x2, blocking collectives: none -> 47.6 us  [body(): lines = lax.all_gather(div.astype(SEND), 'gy', axis=0).astype(F32)]
    all_to_all x5 -> x0, local copies, waits for them, and re-layouts: 40 us -> none  [the longest x3 25.8 us: body(): lax.all_to_all(reordered, 'gy', split_axis=1, concat_axis=2, tiled=True)]
    slice x14 -> x10, local copies, waits for them, and re-layouts: 36.7 us -> 3.7 us  [the longest x4 3.01 us: pieces(): s = lax.slice_in_dim(state, lo, hi, axis=axis + 2)]
  transfers between devices with their start and end apart: 10 -> 6, of which waited for: 2 -> 4; matrix products, arithmetic and copies ran while one was open for 13% -> 6% of each run, Pallas kernels for 0% -> 13%
where the time goes in v1:
time: 254 us; the launch traced here: 253 us
  Pallas kernels  112 us (44%)
  blocking collectives  47.6 us (19%)
  waiting for transfers between devices  33.1 us (13%)
  other arithmetic  27.5 us (11%)
  starting transfers between devices  20.8 us (8%)
  local copies, waits for them, and re-layouts  11.4 us (4%)
    all_gather x2, blocking collectives, body(): lines = lax.all_gather(div.astype(SEND), 'gy', axis=0).astype(F32)  47.6 us
    pallas_call x1, Pallas kernels, stencil(): pl.pallas_call(functools.partial(stencil_kernel, bx, width), grid=(length...  44.1 us
    pallas_call x2, Pallas kernels, transform_x(): pl.pallas_call(x_kernel, out_shape=jax.ShapeDtypeStruct((2, waves, total)...  37 us
    pallas_call x2, Pallas kernels, transform_y(): pl.pallas_call(functools.partial(y_kernel, inner, groups, each), out_shap...  30.7 us
    all_to_all x2, waiting for transfers between devices, body(): lax.all_to_all(waves.astype(SEND), 'gx', split_axis=0, concat_axis=0, til...  26.7 us
    all_to_all x2, starting transfers between devices, body(): lax.all_to_all(waves.astype(SEND), 'gx', split_axis=0, concat_axis=0, til...  17.3 us
    convert_element_type x4, other arithmetic, body(): lines = lax.all_gather(div.astype(SEND), 'gy', axis=0).astype(F32)  8.26 us
    convert_element_type x2, other arithmetic, body(): waves.astype(SEND)  8.09 us
  transfers between devices with their start and end apart: 6, of which 4 were waited for; matrix products, arithmetic and copies ran while one was open for 6% of the time, Pallas kernels for 13%

profile of v1, /device:TPU:13, one launch (start us, length us, event | category | flops | bytes accessed | tf_op | source)
XLA Modules:
  0.0 253.1 jit_solution(15967410043331390001)
XLA Ops:
  0.6 1.1 fusion.1
  1.7 1.8 convert.6
  3.5 1.9 collective-permute-start
  5.5 1.4 fusion
  7.7 1.4 collective-permute-done.xlo
  9.5 3.2 %collective-permute-done.1.xhi = bf16[9,8,2048]{2,1,0:T(8,128)(2,1)S(1)} collective-permute-done((bf16[9,8,2048]{2,1,0:T(8,128)(2,1)S(1)}, bf16[9,8,2048]{2,1,0:T(8,128)(2,1)S(1)}, u32[]{:S(2)}, u32[]{:S(2)}) %collective-permute-start.1) | collective-permute-done | bytes 294944 | tf_op jit(solution)/shard_map/ppermute | solution.py:457
  13.1 1.3 collective-permute-start.2
  14.8 0.6 dynamic-slice_bitcast_fusion.tw
  15.4 1.8 collective-permute-done.3
  17.7 1.0 pad.9.yr
  18.6 0.4 copy.18
  19.1 1.1 pad.8.yl
  20.2 44.1 %stencil.1 = (bf16[4,2,256,2048]{3,2,1,0:T(8,128)(2,1)}, f32[256,2048]{1,0:T(8,128)}, f32[256,2048]{1,0:T(8,128)}) custom-call(bf16[4,2,256,2048]{3,2,1,0:T(8,128)(2,1)} %nxt.1, bf16[4,2,256,2048]{3,2,1,0:T(8,128)(2,1)} %nxt.1, bf16[4,2,256,2048]{3,2,1,0:T(8,128)(2,1)} %nxt.1, s32[256,2048]{1,0:T(8,128)} %h_next.1, s32[256,2048]{1,0:T(8,128)} %h_next.1, ...), custom_call_target="tpu_custom_call" | custom-call | tf_op jit(solution)/shard_map/stencil/pallas_call | solution.py:187
  64.3 1.7 convert_element_type.52
  66.0 22.6 %all-gather.4 = f16[512,2048]{1,0:T(8,128)(2,1)S(1)} all-gather(f16[256,2048]{1,0:T(8,128)(2,1)S(1)} %convert_element_type.52), channel_id=3, replica_groups=mesh['gx'=16,'gy'=2] {'gy'}, dimensions={0}, use_global_device_ids=true | all-gather | bytes 3145728 | tf_op jit(solution)/shard_map/all_gather | solution.py:484
  88.6 2.4 convert.8.f
  91.0 15.4 %transform_y.3 = f32[16,2,2,128,128]{4,3,2,1,0:T(8,128)} custom-call(f32[2,256,2048]{2,1,0:T(8,128)} %convert.8.f, f32[2,16,256]{2,1,0:T(8,128)} %dynamic-slice_bitcast_fusion.tw, bf16[2,256,512]{2,1,0:T(8,128)(2,1)} %constant.34.clone.w), custom_call_target="tpu_custom_call" | custom-call | flops 10000000000 | bytes 10000000 | tf_op jit(solution)/shard_map/transform_y/pallas_call | solution.py:357
  106.4 4.0 %convert_element_type.54 = f16[16,2,2,128,128]{4,3,2,1,0:T(8,128)(2,1)} convert(f32[16,2,2,128,128]{4,3,2,1,0:T(8,128)} %transform_y.3) | non-fusion elementwise | flops 1048576 | bytes 6291456 | tf_op jit(solution)/shard_map/convert_element_type | solution.py:486
  110.4 10.4 %all-to-all-start.1 = ((f16[16,2,2,128,128]{4,3,2,1,0:T(8,128)(2,1)}), f16[16,2,2,128,128]{4,3,2,1,0:T(8,128)(2,1)S(1)}, u32[]{:S(2)}, u32[]{:S(2)}) async-start(f16[16,2,2,128,128]{4,3,2,1,0:T(8,128)(2,1)} %convert_element_type.54), calls=%async_computation.1 | async-start | bytes 4194304 | tf_op jit(solution)/shard_map/all_to_all | solution.py:486
  120.8 1.7 convert_element_type.48
  122.6 25.1 %all-gather.5 = f16[512,2048]{1,0:T(8,128)(2,1)S(1)} all-gather(f16[256,2048]{1,0:T(8,128)(2,1)S(1)} %convert_element_type.48), channel_id=2, replica_groups=mesh['gx'=16,'gy'=2] {'gy'}, dimensions={0}, use_global_device_ids=true | all-gather | bytes 3145728 | tf_op jit(solution)/shard_map/all_gather | solution.py:484
  147.6 2.4 convert.7.f
  150.0 15.4 %transform_y.2 = f32[16,2,2,128,128]{4,3,2,1,0:T(8,128)} custom-call(f32[2,256,2048]{2,1,0:T(8,128)} %convert.7.f, f32[2,16,256]{2,1,0:T(8,128)} %dynamic-slice_bitcast_fusion.tw, bf16[2,256,512]{2,1,0:T(8,128)(2,1)} %constant.34.clone.w), custom_call_target="tpu_custom_call" | custom-call | flops 10000000000 | bytes 10000000 | tf_op jit(solution)/shard_map/transform_y/pallas_call | solution.py:357
  165.4 4.0 %convert_element_type.50 = f16[16,2,2,128,128]{4,3,2,1,0:T(8,128)(2,1)} convert(f32[16,2,2,128,128]{4,3,2,1,0:T(8,128)} %transform_y.2) | non-fusion elementwise | flops 1048576 | bytes 6291456 | tf_op jit(solution)/shard_map/convert_element_type | solution.py:486
  169.4 6.9 %all-to-all-start = ((f16[16,2,2,128,128]{4,3,2,1,0:T(8,128)(2,1)}), f16[16,2,2,128,128]{4,3,2,1,0:T(8,128)(2,1)}, u32[]{:S(2)}, u32[]{:S(2)}) async-start(f16[16,2,2,128,128]{4,3,2,1,0:T(8,128)(2,1)} %convert_element_type.50), calls=%async_computation | async-start | bytes 4194304 | tf_op jit(solution)/shard_map/all_to_all | solution.py:486
  176.3 2.4 convert_element_type.55.z
  178.7 18.4 %transform_x.3 = f32[2,128,4096]{2,1,0:T(8,128)} custom-call(f32[16,2,2,128,128]{4,3,2,1,0:T(8,128)} %convert_element_type.55.z, f32[2,16,256]{2,1,0:T(8,128)} %constant.35.clone.tw, bf16[2,512,512]{2,1,0:T(8,128)(2,1)} %constant.36.clone.v), custom_call_target="tpu_custom_call" | custom-call | flops 10000000000 | bytes 10000000 | tf_op jit(solution)/shard_map/transform_x/pallas_call | solution.py:419
  197.1 26.7 %all-to-all-done = f16[16,2,2,128,128]{4,3,2,1,0:T(8,128)(2,1)} async-done(((f16[16,2,2,128,128]{4,3,2,1,0:T(8,128)(2,1)}), f16[16,2,2,128,128]{4,3,2,1,0:T(8,128)(2,1)}, u32[]{:S(2)}, u32[]{:S(2)}) %all-to-all-start) | async-done | bytes 2097184 | tf_op jit(solution)/shard_map/all_to_all | solution.py:486
  223.8 4.0 %convert_element_type.51.z = f32[16,2,2,128,128]{4,3,2,1,0:T(8,128)} convert(f16[16,2,2,128,128]{4,3,2,1,0:T(8,128)(2,1)} %all-to-all-done) | non-fusion elementwise | flops 1048576 | bytes 6291456 | tf_op jit(solution)/shard_map/convert_element_type | solution.py:487
  227.8 18.6 %transform_x.2 = f32[2,128,4096]{2,1,0:T(8,128)} custom-call(f32[16,2,2,128,128]{4,3,2,1,0:T(8,128)} %convert_element_type.51.z, f32[2,16,256]{2,1,0:T(8,128)} %constant.35.clone.tw, bf16[2,512,512]{2,1,0:T(8,128)(2,1)} %constant.36.clone.v), custom_call_target="tpu_custom_call" | custom-call | flops 10000000000 | bytes 10000000 | tf_op jit(solution)/shard_map/transform_x/pallas_call | solution.py:419
  246.4 2.7 %pad_maximum_fusion = f32[2,2,128,4096]{3,2,0,1:T(8,128)S(1)} fusion(f32[2,1,128,4096]{3,2,0,1:T(8,128)S(1)} %bitcast.22, f32[2,1,128,4096]{3,2,0,1:T(8,128)} %bitcast.23), kind=kLoop, calls=%fused_computation | loop fusion | flops 2097152 | bytes 16777216 | tf_op jit(solution)/shard_map/stack | solution.py:488
  249.1 3.9 %copy.24 = f32[2,2,128,4096]{3,2,1,0:T(8,128)} copy(f32[2,2,128,4096]{3,2,0,1:T(8,128)S(1)} %pad_maximum_fusion) | data formatting | bytes 16777216
  (29 shorter events, 2.5 us)
Async XLA Ops:
  1.7 13.1 %copy-start.3 = (f32[2,2,16,256]{3,2,1,0:T(8,128)S(1)}, f32[2,2,16,256]{3,2,1,0:T(8,128)}, u32[]{:S(2)}) copy-start(f32[2,2,16,256]{3,2,1,0:T(8,128)} %constant.33.clone) | copy-start | bytes 196612
  3.5 5.6 %collective-permute-start = (bf16[9,8,2048]{2,1,0:T(8,128)(2,1)S(1)}, bf16[9,8,2048]{2,1,0:T(8,128)(2,1)S(1)}, u32[]{:S(2)}, u32[]{:S(2)}) collective-permute-start(bf16[9,8,2048]{2,1,0:T(8,128)(2,1)S(1)} %pad_maximum_fusion.1), channel_id=1, source_target_pairs={{0,2},{2,4},{4,6},{6,8},{8,10},{10,12},{12,14},{14,16},{16,18},{18... | collective-permute-start | bytes 884744 | tf_op jit(solution)/shard_map/ppermute | solution.py:457
  5.4 7.2 %collective-permute-start.1 = (bf16[9,8,2048]{2,1,0:T(8,128)(2,1)S(1)}, bf16[9,8,2048]{2,1,0:T(8,128)(2,1)S(1)}, u32[]{:S(2)}, u32[]{:S(2)}) collective-permute-start(bf16[9,8,2048]{2,1,0:T(8,128)(2,1)S(1)} %pad_maximum_fusion.2), channel_id=1, source_target_pairs={{2,0},{4,2},{6,4},{8,6},{10,8},{12,10},{14,12},{16,14},{18,16},{20... | collective-permute-start | bytes 884744 | tf_op jit(solution)/shard_map/ppermute | solution.py:457
  9.1 11.0 %copy-start.1 = (bf16[9,8,2048]{2,1,0:T(8,128)(2,1)}, bf16[9,8,2048]{2,1,0:T(8,128)(2,1)S(1)}, u32[]{:S(2)}) copy-start(bf16[9,8,2048]{2,1,0:T(8,128)(2,1)S(1)} %collective-permute-done.xlo) | copy-start | bytes 884740
  12.6 7.5 %copy-start.2 = (bf16[9,8,2048]{2,1,0:T(8,128)(2,1)}, bf16[9,8,2048]{2,1,0:T(8,128)(2,1)S(1)}, u32[]{:S(2)}) copy-start(bf16[9,8,2048]{2,1,0:T(8,128)(2,1)S(1)} %collective-permute-done.1.xhi) | copy-start | bytes 884740
  13.1 5.5 %collective-permute-start.2 = (bf16[9,272,4]{1,2,0:T(4,128)(2,1)S(1)}, bf16[9,272,4]{1,2,0:T(4,128)(2,1)S(1)}, u32[]{:S(2)}, u32[]{:S(2)}) collective-permute-start(bf16[9,272,4]{1,2,0:T(4,128)(2,1)S(1)} %pad_maximum_fusion.3), channel_id=1, source_target_pairs={{0,1},{1,0},{2,3},{3,2},{4,5},{5,4},{6,7},{7,6},{8,9},{9,8},{10,11... | collective-permute-start | bytes 58760 | tf_op jit(solution)/shard_map/ppermute | solution.py:457
  14.5 2.8 %collective-permute-start.3 = (bf16[9,272,4]{1,2,0:T(4,128)(2,1)S(1)}, bf16[9,272,4]{1,2,0:T(4,128)(2,1)S(1)}, u32[]{:S(2)}, u32[]{:S(2)}) collective-permute-start(bf16[9,272,4]{1,2,0:T(4,128)(2,1)S(1)} %pad_maximum_fusion.4), channel_id=1, source_target_pairs={{1,0},{0,1},{3,2},{2,3},{5,4},{4,5},{7,6},{6,7},{9,8},{8,9},{11,10... | collective-permute-start | bytes 58760 | tf_op jit(solution)/shard_map/ppermute | solution.py:457
  110.4 59.0 %all-to-all-start.1 = ((f16[16,2,2,128,128]{4,3,2,1,0:T(8,128)(2,1)}), f16[16,2,2,128,128]{4,3,2,1,0:T(8,128)(2,1)S(1)}, u32[]{:S(2)}, u32[]{:S(2)}) async-start(f16[16,2,2,128,128]{4,3,2,1,0:T(8,128)(2,1)} %convert_element_type.54), calls=%async_computation.1 | async-start | bytes 4194304 | tf_op jit(solution)/shard_map/all_to_all | solution.py:486
  169.4 54.4 %all-to-all-start = ((f16[16,2,2,128,128]{4,3,2,1,0:T(8,128)(2,1)}), f16[16,2,2,128,128]{4,3,2,1,0:T(8,128)(2,1)}, u32[]{:S(2)}, u32[]{:S(2)}) async-start(f16[16,2,2,128,128]{4,3,2,1,0:T(8,128)(2,1)} %convert_element_type.50), calls=%async_computation | async-start | bytes 4194304 | tf_op jit(solution)/shard_map/all_to_all | solution.py:486
  227.8 18.6 %copy-start = (f32[2,128,4096]{2,1,0:T(8,128)S(1)}, f32[2,128,4096]{2,1,0:T(8,128)}, u32[]{:S(2)}) copy-start(f32[2,128,4096]{2,1,0:T(8,128)} %transform_x.3) | copy-start | bytes 12582916

commit v2 on v1

--- a/solution.py
+++ b/solution.py
@@ -364,12 +364,13 @@
             pltpu.VMEM((RADIX, length, 2 * inner), BF),
         ],
         compiler_params=pltpu.CompilerParams(vmem_limit_bytes=56 * 2**20),
-        cost_estimate=pl.CostEstimate(flops=10**10, bytes_accessed=10**7, transcendentals=0),
+        cost_estimate=pl.CostEstimate(flops=10**11, bytes_accessed=10**7, transcendentals=0),
         name="transform_y",
     )(f, twiddle, matrix)
 
 
-def x_kernel(z, tw, v, out, hi, lo, wide):
+def x_kernel(z, tw, v, *rest):
+    out, hi, lo, wide = rest[-4:]
     count, _, pieces, waves, lanes_each = z.shape
     length = pieces * lanes_each
     inner = wide.shape[1] // count
@@ -411,25 +412,28 @@
     lax.fori_loop(0, wide.shape[1] // 256, turn, 0)
 
 
-def transform_x(z, twiddle, matrix):
+def transform_x(z, twiddle, matrix, level, levels, earlier):
     count, _, pieces, waves, lanes_each = z.shape
     length = pieces * lanes_each
     total = count * length
     padded = max(waves, 128)
     return pl.pallas_call(
         x_kernel,
-        out_shape=jax.ShapeDtypeStruct((2, waves, total), F32),
-        in_specs=[pl.BlockSpec(memory_space=pltpu.VMEM)] * 3,
-        out_specs=pl.BlockSpec(memory_space=pltpu.VMEM),
+        out_shape=jax.ShapeDtypeStruct((2, levels, waves, total), F32),
+        grid=(1,),
+        in_specs=[pl.BlockSpec(memory_space=pltpu.VMEM)] * 3
+        + [pl.BlockSpec(memory_space=pl.ANY)] * len(earlier),
+        out_specs=pl.BlockSpec((2, None, waves, total), lambda i: (0, level, 0, 0)),
+        input_output_aliases={3: 0} if earlier else {},
         scratch_shapes=[
             pltpu.VMEM((count, padded, 2 * length), BF),
             pltpu.VMEM((count, padded, 2 * length), BF),
             pltpu.VMEM((2, total, padded), F32),
         ],
         compiler_params=pltpu.CompilerParams(vmem_limit_bytes=56 * 2**20),
-        cost_estimate=pl.CostEstimate(flops=10**10, bytes_accessed=10**7, transcendentals=0),
+        cost_estimate=pl.CostEstimate(flops=10**11, bytes_accessed=10**7, transcendentals=0),
         name="transform_x",
-    )(z, twiddle, matrix)
+    )(z, twiddle, matrix, *earlier)
 
 
 def tables(count_x, count_y, length, width):
@@ -479,13 +483,27 @@
 
     mine = lax.axis_index("gy")
     twiddle = lax.dynamic_index_in_dim(jnp.asarray(tw_y), mine, 0, keepdims=False)
-    results = []
-    for div in (div0, div1):
-        lines = lax.all_gather(div.astype(SEND), "gy", axis=0).astype(F32)
-        waves = transform_y(lines, twiddle, jnp.asarray(w), count_x, each)
+    swap = [(i, 1 - i) for i in range(count_y)]
+    earlier = ()
+    for level, div in enumerate((div0, div1)):
+        own = div.astype(SEND)
+        if count_y == 2:
+            if level:
+                own, other = lax.optimization_barrier((own, other))
+            other = lax.ppermute(own, "gy", swap)
+            if level:
+                _, own, mixed = lax.optimization_barrier((waves, own, other))
+            else:
+                mixed = other
+            lines = jnp.stack([jnp.where(mine == 0, own, mixed), jnp.where(mine == 0, mixed, own)])
+        else:
+            lines = lax.all_gather(own, "gy", axis=0)
+        waves = transform_y(lines.astype(F32), twiddle, jnp.asarray(w), count_x, each)
         moved = lax.all_to_all(waves.astype(SEND), "gx", split_axis=0, concat_axis=0, tiled=True)
-        results.append(transform_x(moved.astype(F32), jnp.asarray(tw_x), jnp.asarray(v)))
-    return tendency, jnp.stack(results, axis=1)
+        earlier = (
+            transform_x(moved.astype(F32), jnp.asarray(tw_x), jnp.asarray(v), level, levels, earlier),
+        )
+    return tendency, earlier[0]
 
 
 def solution(mesh):

time: 254 us -> 246 us (0.969)
  blocking collectives: 47.6 us -> 0 us
  waiting for transfers between devices: 33.1 us -> 74.7 us
  local copies, waits for them, and re-layouts: 11.4 us -> 7.48 us
    all_gather x2 -> x0, blocking collectives: 47.6 us -> none  [body(): lines = lax.all_gather(div.astype(SEND), 'gy', axis=0).astype(F32)]
    all_to_all x2, waiting for transfers between devices: 26.7 us -> 50.5 us  [body(): lax.all_to_all(waves.astype(SEND), 'gx', split_axis=0, concat_axis=0, til...]
    ppermute x0 -> x2, waiting for transfers between devices: none -> 18.6 us  [body(): other = lax.ppermute(own, 'gy', swap)]
    unnamed x9 -> x8, local copies, waits for them, and re-layouts: 3.96 us -> 0.02 us
    ppermute x0 -> x2, starting transfers between devices: none -> 2.72 us  [body(): other = lax.ppermute(own, 'gy', swap)]
    another operation x2 -> x3, other arithmetic: 4.5 us -> 5.22 us  [the longest x2 3.48 us: body(): jnp.stack([jnp.where(mine == 0, own, mixed), jnp.where(mine == 0, mixed,...]
  transfers between devices with their start and end apart: 6 -> 8, of which waited for: 4 -> 6; matrix products, arithmetic and copies ran while one was open for 6% -> 10% of each run, Pallas kernels for 13% -> 20%
where the time goes in v2:
time: 246 us
  Pallas kernels  112 us (46%)
  waiting for transfers between devices  74.7 us (30%)
  other arithmetic  29.3 us (12%)
  starting transfers between devices  21.6 us (9%)
  local copies, waits for them, and re-layouts  7.48 us (3%)
    all_to_all x2, waiting for transfers between devices, body(): lax.all_to_all(waves.astype(SEND), 'gx', split_axis=0, concat_axis=0, til...  50.5 us
    pallas_call x1, Pallas kernels, stencil(): pl.pallas_call(functools.partial(stencil_kernel, bx, width), grid=(length...  44.1 us
    pallas_call x2, Pallas kernels, transform_x(): pl.pallas_call(x_kernel, out_shape=jax.ShapeDtypeStruct((2, levels, waves...  37 us
    pallas_call x2, Pallas kernels, transform_y(): pl.pallas_call(functools.partial(y_kernel, inner, groups, each), out_shap...  30.7 us
    ppermute x2, waiting for transfers between devices, body(): other = lax.ppermute(own, 'gy', swap)  18.6 us
    all_to_all x2, starting transfers between devices, body(): lax.all_to_all(waves.astype(SEND), 'gx', split_axis=0, concat_axis=0, til...  15.4 us
    convert_element_type x2, other arithmetic, body(): waves.astype(SEND)  8.08 us
    convert_element_type x2, other arithmetic, body(): moved.astype(F32)  6.24 us
  transfers between devices with their start and end apart: 8, of which 6 were waited for; matrix products, arithmetic and copies ran while one was open for 10% of the time, Pallas kernels for 20%

profile of v2, /device:TPU:13, one launch (start us, length us, event | category | flops | bytes accessed | tf_op | source)
XLA Modules:
  0.0 245.6 jit_solution(723425092892057865)
XLA Ops:
  0.6 1.1 fusion.1
  1.7 1.7 convert.6
  3.5 1.9 collective-permute-start
  5.5 1.4 fusion
  7.7 1.4 collective-permute-done.xlo
  9.4 3.2 %collective-permute-done.1.xhi = bf16[9,8,2048]{2,1,0:T(8,128)(2,1)S(1)} collective-permute-done((bf16[9,8,2048]{2,1,0:T(8,128)(2,1)S(1)}, bf16[9,8,2048]{2,1,0:T(8,128)(2,1)S(1)}, u32[]{:S(2)}, u32[]{:S(2)}) %collective-permute-start.1) | collective-permute-done | bytes 294944 | tf_op jit(solution)/shard_map/ppermute | solution.py:461
  13.1 1.3 collective-permute-start.3
  14.7 1.1 collective-permute-done.3
  16.2 1.0 pad.9.yr
  17.6 1.1 pad.8.yl
  18.7 44.1 %stencil.1 = (bf16[4,2,256,2048]{3,2,1,0:T(8,128)(2,1)}, f32[256,2048]{1,0:T(8,128)}, f32[256,2048]{1,0:T(8,128)}) custom-call(bf16[4,2,256,2048]{3,2,1,0:T(8,128)(2,1)} %nxt.1, bf16[4,2,256,2048]{3,2,1,0:T(8,128)(2,1)} %nxt.1, bf16[4,2,256,2048]{3,2,1,0:T(8,128)(2,1)} %nxt.1, s32[256,2048]{1,0:T(8,128)} %h_next.1, s32[256,2048]{1,0:T(8,128)} %h_next.1, ...), custom_call_target="tpu_custom_call" | custom-call | tf_op jit(solution)/shard_map/stencil/pallas_call | solution.py:187
  62.8 2.8 %convert_element_type.48 = f16[256,2048]{1,0:T(8,128)(2,1)} convert(f32[256,2048]{1,0:T(8,128)} %get-tuple-element.9) | non-fusion elementwise | flops 524288 | bytes 3145728 | tf_op jit(solution)/shard_map/convert_element_type | solution.py:489
  65.6 1.2 collective-permute-start.4
  67.4 1.7 convert_element_type.50
  69.2 18.6 %collective-permute-done.4 = f16[256,2048]{1,0:T(8,128)(2,1)} collective-permute-done((f16[256,2048]{1,0:T(8,128)(2,1)}, f16[256,2048]{1,0:T(8,128)(2,1)}, u32[]{:S(2)}, u32[]{:S(2)}) %collective-permute-start.4) | collective-permute-done | bytes 1048608 | tf_op jit(solution)/shard_map/ppermute | solution.py:493
  87.8 1.5 collective-permute-start.5
  89.3 1.7 select_bitcast_fusion.3
  91.0 2.5 %maximum_convert_fusion.f = f32[2,256,2048]{2,1,0:T(8,128)} fusion(f16[1,256,2048]{2,1,0:T(8,128)(2,1)S(1)} %get-tuple-element.21, f16[1,256,2048]{2,1,0:T(8,128)(2,1)S(1)} %get-tuple-element.20), kind=kLoop, calls=%fused_computation | loop fusion | flops 2097152 | bytes 6291456 | tf_op jit(solution)/shard_map/convert_element_type | solution.py:501
  93.5 15.3 %transform_y.2 = f32[16,2,2,128,128]{4,3,2,1,0:T(8,128)} custom-call(f32[2,256,2048]{2,1,0:T(8,128)} %maximum_convert_fusion.f, f32[2,16,256]{2,1,0:T(8,128)} %dynamic-slice_bitcast_fusion.tw, bf16[2,256,512]{2,1,0:T(8,128)(2,1)} %constant.34.clone.w), custom_call_target="tpu_custom_call" | custom-call | flops 99999997952 | bytes 10000000 | tf_op jit(solution)/shard_map/transform_y/pallas_call | solution.py:357
  108.9 4.0 %convert_element_type.54 = f16[16,2,2,128,128]{4,3,2,1,0:T(8,128)(2,1)} convert(f32[16,2,2,128,128]{4,3,2,1,0:T(8,128)} %transform_y.2) | non-fusion elementwise | flops 1048576 | bytes 6291456 | tf_op jit(solution)/shard_map/convert_element_type | solution.py:502
  112.9 10.5 %all-to-all-start.1 = ((f16[16,2,2,128,128]{4,3,2,1,0:T(8,128)(2,1)}), f16[16,2,2,128,128]{4,3,2,1,0:T(8,128)(2,1)S(1)}, u32[]{:S(2)}, u32[]{:S(2)}) async-start(f16[16,2,2,128,128]{4,3,2,1,0:T(8,128)(2,1)} %convert_element_type.54), calls=%async_computation.1 | async-start | bytes 4194304 | tf_op jit(solution)/shard_map/all_to_all | solution.py:502
  123.4 1.8 select_bitcast_fusion.1
  125.1 2.5 %maximum_convert_fusion.1.f = f32[2,256,2048]{2,1,0:T(8,128)} fusion(f16[1,256,2048]{2,1,0:T(8,128)(2,1)S(1)} %get-tuple-element.19, f16[1,256,2048]{2,1,0:T(8,128)(2,1)S(1)} %get-tuple-element.18), kind=kLoop, calls=%fused_computation.1 | loop fusion | flops 2097152 | bytes 6291456 | tf_op jit(solution)/shard_map/convert_element_type | solution.py:501
  127.6 15.3 %transform_y.3 = f32[16,2,2,128,128]{4,3,2,1,0:T(8,128)} custom-call(f32[2,256,2048]{2,1,0:T(8,128)} %maximum_convert_fusion.1.f, f32[2,16,256]{2,1,0:T(8,128)} %dynamic-slice_bitcast_fusion.tw, bf16[2,256,512]{2,1,0:T(8,128)(2,1)} %constant.34.clone.w), custom_call_target="tpu_custom_call" | custom-call | flops 99999997952 | bytes 10000000 | tf_op jit(solution)/shard_map/transform_y/pallas_call | solution.py:357
  143.0 4.0 %convert_element_type.52 = f16[16,2,2,128,128]{4,3,2,1,0:T(8,128)(2,1)} convert(f32[16,2,2,128,128]{4,3,2,1,0:T(8,128)} %transform_y.3) | non-fusion elementwise | flops 1048576 | bytes 6291456 | tf_op jit(solution)/shard_map/convert_element_type | solution.py:502
  147.0 23.7 %all-to-all-done.1 = f16[16,2,2,128,128]{4,3,2,1,0:T(8,128)(2,1)S(1)} async-done(((f16[16,2,2,128,128]{4,3,2,1,0:T(8,128)(2,1)}), f16[16,2,2,128,128]{4,3,2,1,0:T(8,128)(2,1)S(1)}, u32[]{:S(2)}, u32[]{:S(2)}) %all-to-all-start.1) | async-done | bytes 2097184 | tf_op jit(solution)/shard_map/all_to_all | solution.py:502
  170.8 4.9 %all-to-all-start = ((f16[16,2,2,128,128]{4,3,2,1,0:T(8,128)(2,1)}), f16[16,2,2,128,128]{4,3,2,1,0:T(8,128)(2,1)}, u32[]{:S(2)}, u32[]{:S(2)}) async-start(f16[16,2,2,128,128]{4,3,2,1,0:T(8,128)(2,1)} %convert_element_type.52), calls=%async_computation | async-start | bytes 4194304 | tf_op jit(solution)/shard_map/all_to_all | solution.py:502
  175.7 2.3 convert_element_type.55.z
  178.0 18.5 %transform_x.2.rest_0_ = f32[2,2,128,4096]{3,2,1,0:T(8,128)} custom-call(f32[16,2,2,128,128]{4,3,2,1,0:T(8,128)} %convert_element_type.55.z, f32[2,16,256]{2,1,0:T(8,128)} %constant.35.clone.tw, bf16[2,512,512]{2,1,0:T(8,128)(2,1)} %constant.36.clone.v), custom_call_target="tpu_custom_call" | custom-call | flops 99999997952 | bytes 10000000 | tf_op jit(solution)/shard_map/transform_x/pallas_call | solution.py:420
  196.5 26.7 %all-to-all-done = f16[16,2,2,128,128]{4,3,2,1,0:T(8,128)(2,1)} async-done(((f16[16,2,2,128,128]{4,3,2,1,0:T(8,128)(2,1)}), f16[16,2,2,128,128]{4,3,2,1,0:T(8,128)(2,1)}, u32[]{:S(2)}, u32[]{:S(2)}) %all-to-all-start) | async-done | bytes 2097184 | tf_op jit(solution)/shard_map/all_to_all | solution.py:502
  223.2 3.9 %convert_element_type.53.z = f32[16,2,2,128,128]{4,3,2,1,0:T(8,128)} convert(f16[16,2,2,128,128]{4,3,2,1,0:T(8,128)(2,1)} %all-to-all-done) | non-fusion elementwise | flops 1048576 | bytes 6291456 | tf_op jit(solution)/shard_map/convert_element_type | solution.py:504
  227.1 18.5 %transform_x.3 = f32[2,2,128,4096]{3,2,1,0:T(8,128)} custom-call(f32[16,2,2,128,128]{4,3,2,1,0:T(8,128)} %convert_element_type.53.z, f32[2,16,256]{2,1,0:T(8,128)} %constant.35.clone.tw, bf16[2,512,512]{2,1,0:T(8,128)(2,1)} %constant.36.clone.v, f32[2,2,128,4096]{3,2,1,0:T(8,128)} %transform_x.2.rest_0_), custom_call_target="tpu_custom_call", output_to_operand_aliasing={{}: (3, {})} | custom-call | flops 99999997952 | bytes 10000000 | tf_op jit(solution)/shard_map/transform_x/pallas_call | solution.py:420
  (31 shorter events, 3.6 us)
Async XLA Ops:
  3.5 5.6 %collective-permute-start = (bf16[9,8,2048]{2,1,0:T(8,128)(2,1)S(1)}, bf16[9,8,2048]{2,1,0:T(8,128)(2,1)S(1)}, u32[]{:S(2)}, u32[]{:S(2)}) collective-permute-start(bf16[9,8,2048]{2,1,0:T(8,128)(2,1)S(1)} %pad_maximum_fusion), channel_id=1, source_target_pairs={{0,2},{2,4},{4,6},{6,8},{8,10},{10,12},{12,14},{14,16},{16,18},{18... | collective-permute-start | bytes 884744 | tf_op jit(solution)/shard_map/ppermute | solution.py:461
  5.4 7.2 %collective-permute-start.1 = (bf16[9,8,2048]{2,1,0:T(8,128)(2,1)S(1)}, bf16[9,8,2048]{2,1,0:T(8,128)(2,1)S(1)}, u32[]{:S(2)}, u32[]{:S(2)}) collective-permute-start(bf16[9,8,2048]{2,1,0:T(8,128)(2,1)S(1)} %pad_maximum_fusion.1), channel_id=1, source_target_pairs={{2,0},{4,2},{6,4},{8,6},{10,8},{12,10},{14,12},{16,14},{18,16},{20... | collective-permute-start | bytes 884744 | tf_op jit(solution)/shard_map/ppermute | solution.py:461
  9.1 9.6 %copy-start.1 = (bf16[9,8,2048]{2,1,0:T(8,128)(2,1)}, bf16[9,8,2048]{2,1,0:T(8,128)(2,1)S(1)}, u32[]{:S(2)}) copy-start(bf16[9,8,2048]{2,1,0:T(8,128)(2,1)S(1)} %collective-permute-done.xlo) | copy-start | bytes 884740
  12.6 6.1 %copy-start.2 = (bf16[9,8,2048]{2,1,0:T(8,128)(2,1)}, bf16[9,8,2048]{2,1,0:T(8,128)(2,1)S(1)}, u32[]{:S(2)}) copy-start(bf16[9,8,2048]{2,1,0:T(8,128)(2,1)S(1)} %collective-permute-done.1.xhi) | copy-start | bytes 884740
  13.1 2.8 %collective-permute-start.3 = (bf16[9,272,4]{1,2,0:T(4,128)(2,1)S(1)}, bf16[9,272,4]{1,2,0:T(4,128)(2,1)S(1)}, u32[]{:S(2)}, u32[]{:S(2)}) collective-permute-start(bf16[9,272,4]{1,2,0:T(4,128)(2,1)S(1)} %pad_maximum_fusion.3), channel_id=1, source_target_pairs={{1,0},{0,1},{3,2},{2,3},{5,4},{4,5},{7,6},{6,7},{9,8},{8,9},{11,10... | collective-permute-start | bytes 58760 | tf_op jit(solution)/shard_map/ppermute | solution.py:461
  14.4 2.8 %collective-permute-start.2 = (bf16[9,272,4]{1,2,0:T(4,128)(2,1)S(1)}, bf16[9,272,4]{1,2,0:T(4,128)(2,1)S(1)}, u32[]{:S(2)}, u32[]{:S(2)}) collective-permute-start(bf16[9,272,4]{1,2,0:T(4,128)(2,1)S(1)} %pad_maximum_fusion.2), channel_id=1, source_target_pairs={{0,1},{1,0},{2,3},{3,2},{4,5},{5,4},{6,7},{7,6},{8,9},{9,8},{10,11... | collective-permute-start | bytes 58760 | tf_op jit(solution)/shard_map/ppermute | solution.py:461
  62.8 4.0 %copy-start.3 = (f32[2,2,16,256]{3,2,1,0:T(8,128)S(1)}, f32[2,2,16,256]{3,2,1,0:T(8,128)}, u32[]{:S(2)}) copy-start(f32[2,2,16,256]{3,2,1,0:T(8,128)} %constant.33.clone) | copy-start | bytes 196612
  65.6 23.7 %copy-start = (f32[256,2048]{1,0:T(8,128)S(1)}, f32[256,2048]{1,0:T(8,128)}, u32[]{:S(2)}) copy-start(f32[256,2048]{1,0:T(8,128)} %get-tuple-element.9) | copy-start | bytes 6291460
  65.6 22.2 %collective-permute-start.4 = (f16[256,2048]{1,0:T(8,128)(2,1)}, f16[256,2048]{1,0:T(8,128)(2,1)}, u32[]{:S(2)}, u32[]{:S(2)}) collective-permute-start(f16[256,2048]{1,0:T(8,128)(2,1)} %convert_element_type.48), channel_id=1, source_target_pairs={{0,1},{1,0},{2,3},{3,2},{4,5},{5,4},{6,7},{7,6},{8,9},{9,8},{10,11... | collective-permute-start | bytes 3145736 | tf_op jit(solution)/shard_map/ppermute | solution.py:493
  87.8 35.5 %collective-permute-start.5 = (f16[256,2048]{1,0:T(8,128)(2,1)S(1)}, f16[256,2048]{1,0:T(8,128)(2,1)}, u32[]{:S(2)}, u32[]{:S(2)}) collective-permute-start(f16[256,2048]{1,0:T(8,128)(2,1)S(1)} %convert_element_type.50), channel_id=1, source_target_pairs={{0,1},{1,0},{2,3},{3,2},{4,5},{5,4},{6,7},{7,6},{8,9},{9,8},{10,11... | collective-permute-start | bytes 3145736 | tf_op jit(solution)/shard_map/ppermute | solution.py:493
  112.9 57.9 %all-to-all-start.1 = ((f16[16,2,2,128,128]{4,3,2,1,0:T(8,128)(2,1)}), f16[16,2,2,128,128]{4,3,2,1,0:T(8,128)(2,1)S(1)}, u32[]{:S(2)}, u32[]{:S(2)}) async-start(f16[16,2,2,128,128]{4,3,2,1,0:T(8,128)(2,1)} %convert_element_type.54), calls=%async_computation.1 | async-start | bytes 4194304 | tf_op jit(solution)/shard_map/all_to_all | solution.py:502
  170.8 52.4 %all-to-all-start = ((f16[16,2,2,128,128]{4,3,2,1,0:T(8,128)(2,1)}), f16[16,2,2,128,128]{4,3,2,1,0:T(8,128)(2,1)}, u32[]{:S(2)}, u32[]{:S(2)}) async-start(f16[16,2,2,128,128]{4,3,2,1,0:T(8,128)(2,1)} %convert_element_type.52), calls=%async_computation | async-start | bytes 4194304 | tf_op jit(solution)/shard_map/all_to_all | solution.py:502

commit v3 on v2

--- a/solution.py
+++ b/solution.py
@@ -43,7 +43,7 @@
     bx, width,
     main, prev, nxt, heights, h_prev, h_next, flag, xlo, xhi, yl, yr, dy, dx, sy, sx,
     tend, div0, div1,
-    m_s, h_s, t_s,
+    m_s, h_s, t_s, every,
 ):
     i = pl.program_id(0)
     last = pl.num_programs(0) - 1
@@ -88,10 +88,9 @@
                 h <= float(f % 2), ref[f, side, :].astype(F32), 0.0
             ).astype(BF)
 
-    def tendency(f, lanes, window, matrix, centers, fluids, n):
+    def tendency(f, lanes, along_y, centers, n):
         k = f % 2
         mid = m_s[f, :, lanes]
-        along_y = dot(m_s[f, :, window], matrix)
         along_x = dot(dx[...], mid)
         other = m_s[f + 1 - 2 * k, :, lanes].astype(F32)
         u60, v60, wz = centers[k]
@@ -120,10 +119,11 @@
         fluids = [(h <= float(k)).astype(F32) for k in range(2)]
         shine = flag[:, outs].astype(F32)
         stars = []
+        every[...] = dot(m_s[:, :, window].reshape(8 * rows, 512), dy[...])
         for k in range(2):
             for c in (0, 1, 2, 3):
                 f = 2 * c + k
-                t = tendency(f, lanes, window, dy[...], centers, fluids, 256)
+                t = tendency(f, lanes, every[f * rows : (f + 1) * rows, :], centers, 256)
                 if c == 2:
                     t = t + BETA * m_s[6 + k, :, lanes].astype(F32)
                 if c == 3:
@@ -155,7 +155,7 @@
         centers = centers_of(target)
         h = h_s[:, target]
         for k in range(2):
-            t = tendency(2 + k, target, window, matrix, centers, None, 128)
+            t = tendency(2 + k, target, dot(m_s[2 + k, :, window], matrix), centers, 128)
             t_s[k, :, target] = jnp.where(h <= float(k), t, 0.0).astype(BF)
 
     def second(j, carry):
@@ -218,6 +218,7 @@
             pltpu.VMEM((8, rows, ext), BF),
             pltpu.VMEM((rows, ext), F32),
             pltpu.VMEM((2, rows, ext), BF),
+            pltpu.VMEM((8 * rows, 512), F32),
         ],
         compiler_params=pltpu.CompilerParams(vmem_limit_bytes=56 * 2**20),
         name="stencil",
@@ -299,7 +300,7 @@
     full = np.block([[c, s], [-s, c]])
     high = full.astype(np.float32).astype(jnp.bfloat16)
     low = (full - high.astype(np.float64)).astype(jnp.bfloat16)
-    return np.stack([high, low])
+    return np.concatenate([high, low])
 
 
 def y_kernel(inner, groups, each, f, tw, w, out, hi, lo):
@@ -338,7 +339,9 @@
 
     def multiply(t, carry):
         h = hi[t]
-        got = dot_t(w[0], h) + dot_t(w[0], lo[t]) + dot_t(w[1], h)
+        both = dot_t(w[...], h)
+        n = w.shape[0] // 2
+        got = both[:n] + both[n:] + dot_t(w[:n, :], lo[t])
         for part in range(2):
             for g in range(groups):
                 base = (part * groups + g) * each
@@ -396,7 +399,9 @@
 
     def multiply(t, carry):
         h = hi[t]
-        got = dot_t(v[0], h) + dot_t(v[0], lo[t]) + dot_t(v[1], h)
+        both = dot_t(v[...], h)
+        n = v.shape[0] // 2
+        got = both[:n] + both[n:] + dot_t(v[:n, :], lo[t])
         for part in range(2):
             wide[part, pl.ds(t, inner, stride=count), :] = got[part * inner : (part + 1) * inner]
         return carry

time: 246 us -> 244 us (level)
  Pallas kernels: 112 us -> 109 us
where the time goes in v3:
time: 244 us; the launch traced here: 243 us
  Pallas kernels  109 us (45%)
  waiting for transfers between devices  74.8 us (31%)
  other arithmetic  29.3 us (12%)
  starting transfers between devices  21.6 us (9%)
  local copies, waits for them, and re-layouts  7.48 us (3%)
    all_to_all x2, waiting for transfers between devices, body(): lax.all_to_all(waves.astype(SEND), 'gx', split_axis=0, concat_axis=0, til...  50.6 us
    pallas_call x1, Pallas kernels, stencil(): pl.pallas_call(functools.partial(stencil_kernel, bx, width), grid=(length...  42 us
    pallas_call x2, Pallas kernels, transform_x(): pl.pallas_call(x_kernel, out_shape=jax.ShapeDtypeStruct((2, levels, waves...  36.8 us
    pallas_call x2, Pallas kernels, transform_y(): pl.pallas_call(functools.partial(y_kernel, inner, groups, each), out_shap...  30.6 us
    ppermute x2, waiting for transfers between devices, body(): other = lax.ppermute(own, 'gy', swap)  18.6 us
    all_to_all x2, starting transfers between devices, body(): lax.all_to_all(waves.astype(SEND), 'gx', split_axis=0, concat_axis=0, til...  15.4 us
    convert_element_type x2, other arithmetic, body(): waves.astype(SEND)  8.08 us
    convert_element_type x2, other arithmetic, body(): moved.astype(F32)  6.24 us
  transfers between devices with their start and end apart: 8, of which 6 were waited for; matrix products, arithmetic and copies ran while one was open for 10% of the time, Pallas kernels for 20%

profile of v3, /device:TPU:13, one launch (start us, length us, event | category | flops | bytes accessed | tf_op | source)
XLA Modules:
  0.0 243.3 jit_solution(12531477290455564226)
XLA Ops:
  0.6 1.1 fusion.1
  1.7 1.7 convert.6
  3.5 1.9 collective-permute-start
  5.5 1.4 fusion
  7.7 1.4 collective-permute-done.xlo
  9.4 3.2 %collective-permute-done.1.xhi = bf16[9,8,2048]{2,1,0:T(8,128)(2,1)S(1)} collective-permute-done((bf16[9,8,2048]{2,1,0:T(8,128)(2,1)S(1)}, bf16[9,8,2048]{2,1,0:T(8,128)(2,1)S(1)}, u32[]{:S(2)}, u32[]{:S(2)}) %collective-permute-start.1) | collective-permute-done | bytes 294944 | tf_op jit(solution)/shard_map/ppermute | solution.py:466
  13.1 1.3 collective-permute-start.3
  14.7 1.1 collective-permute-done.3
  16.2 1.0 pad.9.yr
  17.6 1.1 pad.8.yl
  18.7 42.0 %stencil.1 = (bf16[4,2,256,2048]{3,2,1,0:T(8,128)(2,1)}, f32[256,2048]{1,0:T(8,128)}, f32[256,2048]{1,0:T(8,128)}) custom-call(bf16[4,2,256,2048]{3,2,1,0:T(8,128)(2,1)} %nxt.1, bf16[4,2,256,2048]{3,2,1,0:T(8,128)(2,1)} %nxt.1, bf16[4,2,256,2048]{3,2,1,0:T(8,128)(2,1)} %nxt.1, s32[256,2048]{1,0:T(8,128)} %h_next.1, s32[256,2048]{1,0:T(8,128)} %h_next.1, ...), custom_call_target="tpu_custom_call" | custom-call | tf_op jit(solution)/shard_map/stencil/pallas_call | solution.py:187
  60.7 2.8 %convert_element_type.48 = f16[256,2048]{1,0:T(8,128)(2,1)} convert(f32[256,2048]{1,0:T(8,128)} %get-tuple-element.9) | non-fusion elementwise | flops 524288 | bytes 3145728 | tf_op jit(solution)/shard_map/convert_element_type | solution.py:494
  63.4 1.2 collective-permute-start.4
  65.3 1.7 convert_element_type.50
  67.0 18.6 %collective-permute-done.4 = f16[256,2048]{1,0:T(8,128)(2,1)} collective-permute-done((f16[256,2048]{1,0:T(8,128)(2,1)}, f16[256,2048]{1,0:T(8,128)(2,1)}, u32[]{:S(2)}, u32[]{:S(2)}) %collective-permute-start.4) | collective-permute-done | bytes 1048608 | tf_op jit(solution)/shard_map/ppermute | solution.py:498
  85.7 1.5 collective-permute-start.5
  87.2 1.7 select_bitcast_fusion.3
  88.9 2.5 %maximum_convert_fusion.f = f32[2,256,2048]{2,1,0:T(8,128)} fusion(f16[1,256,2048]{2,1,0:T(8,128)(2,1)S(1)} %get-tuple-element.21, f16[1,256,2048]{2,1,0:T(8,128)(2,1)S(1)} %get-tuple-element.20), kind=kLoop, calls=%fused_computation | loop fusion | flops 2097152 | bytes 6291456 | tf_op jit(solution)/shard_map/convert_element_type | solution.py:506
  91.4 15.3 %transform_y.2 = f32[16,2,2,128,128]{4,3,2,1,0:T(8,128)} custom-call(f32[2,256,2048]{2,1,0:T(8,128)} %maximum_convert_fusion.f, f32[2,16,256]{2,1,0:T(8,128)} %dynamic-slice_bitcast_fusion.tw, bf16[512,512]{1,0:T(8,128)(2,1)} %constant.34.clone.w), custom_call_target="tpu_custom_call" | custom-call | flops 99999997952 | bytes 10000000 | tf_op jit(solution)/shard_map/transform_y/pallas_call | solution.py:360
  106.7 4.0 %convert_element_type.54 = f16[16,2,2,128,128]{4,3,2,1,0:T(8,128)(2,1)} convert(f32[16,2,2,128,128]{4,3,2,1,0:T(8,128)} %transform_y.2) | non-fusion elementwise | flops 1048576 | bytes 6291456 | tf_op jit(solution)/shard_map/convert_element_type | solution.py:507
  110.7 10.4 %all-to-all-start.1 = ((f16[16,2,2,128,128]{4,3,2,1,0:T(8,128)(2,1)}), f16[16,2,2,128,128]{4,3,2,1,0:T(8,128)(2,1)S(1)}, u32[]{:S(2)}, u32[]{:S(2)}) async-start(f16[16,2,2,128,128]{4,3,2,1,0:T(8,128)(2,1)} %convert_element_type.54), calls=%async_computation.1 | async-start | bytes 4194304 | tf_op jit(solution)/shard_map/all_to_all | solution.py:507
  121.2 1.8 select_bitcast_fusion.1
  122.9 2.5 %maximum_convert_fusion.1.f = f32[2,256,2048]{2,1,0:T(8,128)} fusion(f16[1,256,2048]{2,1,0:T(8,128)(2,1)S(1)} %get-tuple-element.19, f16[1,256,2048]{2,1,0:T(8,128)(2,1)S(1)} %get-tuple-element.18), kind=kLoop, calls=%fused_computation.1 | loop fusion | flops 2097152 | bytes 6291456 | tf_op jit(solution)/shard_map/convert_element_type | solution.py:506
  125.4 15.3 %transform_y.3 = f32[16,2,2,128,128]{4,3,2,1,0:T(8,128)} custom-call(f32[2,256,2048]{2,1,0:T(8,128)} %maximum_convert_fusion.1.f, f32[2,16,256]{2,1,0:T(8,128)} %dynamic-slice_bitcast_fusion.tw, bf16[512,512]{1,0:T(8,128)(2,1)} %constant.34.clone.w), custom_call_target="tpu_custom_call" | custom-call | flops 99999997952 | bytes 10000000 | tf_op jit(solution)/shard_map/transform_y/pallas_call | solution.py:360
  140.8 4.0 %convert_element_type.52 = f16[16,2,2,128,128]{4,3,2,1,0:T(8,128)(2,1)} convert(f32[16,2,2,128,128]{4,3,2,1,0:T(8,128)} %transform_y.3) | non-fusion elementwise | flops 1048576 | bytes 6291456 | tf_op jit(solution)/shard_map/convert_element_type | solution.py:507
  144.8 23.8 %all-to-all-done.1 = f16[16,2,2,128,128]{4,3,2,1,0:T(8,128)(2,1)S(1)} async-done(((f16[16,2,2,128,128]{4,3,2,1,0:T(8,128)(2,1)}), f16[16,2,2,128,128]{4,3,2,1,0:T(8,128)(2,1)S(1)}, u32[]{:S(2)}, u32[]{:S(2)}) %all-to-all-start.1) | async-done | bytes 2097184 | tf_op jit(solution)/shard_map/all_to_all | solution.py:507
  168.6 4.9 %all-to-all-start = ((f16[16,2,2,128,128]{4,3,2,1,0:T(8,128)(2,1)}), f16[16,2,2,128,128]{4,3,2,1,0:T(8,128)(2,1)}, u32[]{:S(2)}, u32[]{:S(2)}) async-start(f16[16,2,2,128,128]{4,3,2,1,0:T(8,128)(2,1)} %convert_element_type.52), calls=%async_computation | async-start | bytes 4194304 | tf_op jit(solution)/shard_map/all_to_all | solution.py:507
  173.5 2.3 convert_element_type.55.z
  175.8 18.4 %transform_x.2.rest_0_ = f32[2,2,128,4096]{3,2,1,0:T(8,128)} custom-call(f32[16,2,2,128,128]{4,3,2,1,0:T(8,128)} %convert_element_type.55.z, f32[2,16,256]{2,1,0:T(8,128)} %constant.35.clone.tw, bf16[1024,512]{1,0:T(8,128)(2,1)} %constant.36.clone.v), custom_call_target="tpu_custom_call" | custom-call | flops 99999997952 | bytes 10000000 | tf_op jit(solution)/shard_map/transform_x/pallas_call | solution.py:425
  194.2 26.8 %all-to-all-done = f16[16,2,2,128,128]{4,3,2,1,0:T(8,128)(2,1)} async-done(((f16[16,2,2,128,128]{4,3,2,1,0:T(8,128)(2,1)}), f16[16,2,2,128,128]{4,3,2,1,0:T(8,128)(2,1)}, u32[]{:S(2)}, u32[]{:S(2)}) %all-to-all-start) | async-done | bytes 2097184 | tf_op jit(solution)/shard_map/all_to_all | solution.py:507
  221.0 3.9 %convert_element_type.53.z = f32[16,2,2,128,128]{4,3,2,1,0:T(8,128)} convert(f16[16,2,2,128,128]{4,3,2,1,0:T(8,128)(2,1)} %all-to-all-done) | non-fusion elementwise | flops 1048576 | bytes 6291456 | tf_op jit(solution)/shard_map/convert_element_type | solution.py:509
  224.9 18.4 %transform_x.3 = f32[2,2,128,4096]{3,2,1,0:T(8,128)} custom-call(f32[16,2,2,128,128]{4,3,2,1,0:T(8,128)} %convert_element_type.53.z, f32[2,16,256]{2,1,0:T(8,128)} %constant.35.clone.tw, bf16[1024,512]{1,0:T(8,128)(2,1)} %constant.36.clone.v, f32[2,2,128,4096]{3,2,1,0:T(8,128)} %transform_x.2.rest_0_), custom_call_target="tpu_custom_call", output_to_operand_aliasing={{}: (3, {})} | custom-call | flops 99999997952 | bytes 10000000 | tf_op jit(solution)/shard_map/transform_x/pallas_call | solution.py:425
  (31 shorter events, 3.6 us)
Async XLA Ops:
  3.5 5.6 %collective-permute-start = (bf16[9,8,2048]{2,1,0:T(8,128)(2,1)S(1)}, bf16[9,8,2048]{2,1,0:T(8,128)(2,1)S(1)}, u32[]{:S(2)}, u32[]{:S(2)}) collective-permute-start(bf16[9,8,2048]{2,1,0:T(8,128)(2,1)S(1)} %pad_maximum_fusion), channel_id=1, source_target_pairs={{0,2},{2,4},{4,6},{6,8},{8,10},{10,12},{12,14},{14,16},{16,18},{18... | collective-permute-start | bytes 884744 | tf_op jit(solution)/shard_map/ppermute | solution.py:466
  5.4 7.2 %collective-permute-start.1 = (bf16[9,8,2048]{2,1,0:T(8,128)(2,1)S(1)}, bf16[9,8,2048]{2,1,0:T(8,128)(2,1)S(1)}, u32[]{:S(2)}, u32[]{:S(2)}) collective-permute-start(bf16[9,8,2048]{2,1,0:T(8,128)(2,1)S(1)} %pad_maximum_fusion.1), channel_id=1, source_target_pairs={{2,0},{4,2},{6,4},{8,6},{10,8},{12,10},{14,12},{16,14},{18,16},{20... | collective-permute-start | bytes 884744 | tf_op jit(solution)/shard_map/ppermute | solution.py:466
  9.1 9.6 %copy-start.1 = (bf16[9,8,2048]{2,1,0:T(8,128)(2,1)}, bf16[9,8,2048]{2,1,0:T(8,128)(2,1)S(1)}, u32[]{:S(2)}) copy-start(bf16[9,8,2048]{2,1,0:T(8,128)(2,1)S(1)} %collective-permute-done.xlo) | copy-start | bytes 884740
  12.6 6.1 %copy-start.2 = (bf16[9,8,2048]{2,1,0:T(8,128)(2,1)}, bf16[9,8,2048]{2,1,0:T(8,128)(2,1)S(1)}, u32[]{:S(2)}) copy-start(bf16[9,8,2048]{2,1,0:T(8,128)(2,1)S(1)} %collective-permute-done.1.xhi) | copy-start | bytes 884740
  13.1 2.8 %collective-permute-start.3 = (bf16[9,272,4]{1,2,0:T(4,128)(2,1)S(1)}, bf16[9,272,4]{1,2,0:T(4,128)(2,1)S(1)}, u32[]{:S(2)}, u32[]{:S(2)}) collective-permute-start(bf16[9,272,4]{1,2,0:T(4,128)(2,1)S(1)} %pad_maximum_fusion.3), channel_id=1, source_target_pairs={{1,0},{0,1},{3,2},{2,3},{5,4},{4,5},{7,6},{6,7},{9,8},{8,9},{11,10... | collective-permute-start | bytes 58760 | tf_op jit(solution)/shard_map/ppermute | solution.py:466
  14.4 2.8 %collective-permute-start.2 = (bf16[9,272,4]{1,2,0:T(4,128)(2,1)S(1)}, bf16[9,272,4]{1,2,0:T(4,128)(2,1)S(1)}, u32[]{:S(2)}, u32[]{:S(2)}) collective-permute-start(bf16[9,272,4]{1,2,0:T(4,128)(2,1)S(1)} %pad_maximum_fusion.2), channel_id=1, source_target_pairs={{0,1},{1,0},{2,3},{3,2},{4,5},{5,4},{6,7},{7,6},{8,9},{9,8},{10,11... | collective-permute-start | bytes 58760 | tf_op jit(solution)/shard_map/ppermute | solution.py:466
  60.7 4.0 %copy-start.3 = (f32[2,2,16,256]{3,2,1,0:T(8,128)S(1)}, f32[2,2,16,256]{3,2,1,0:T(8,128)}, u32[]{:S(2)}) copy-start(f32[2,2,16,256]{3,2,1,0:T(8,128)} %constant.33.clone) | copy-start | bytes 196612
  63.4 23.7 %copy-start = (f32[256,2048]{1,0:T(8,128)S(1)}, f32[256,2048]{1,0:T(8,128)}, u32[]{:S(2)}) copy-start(f32[256,2048]{1,0:T(8,128)} %get-tuple-element.9) | copy-start | bytes 6291460
  63.4 22.2 %collective-permute-start.4 = (f16[256,2048]{1,0:T(8,128)(2,1)}, f16[256,2048]{1,0:T(8,128)(2,1)}, u32[]{:S(2)}, u32[]{:S(2)}) collective-permute-start(f16[256,2048]{1,0:T(8,128)(2,1)} %convert_element_type.48), channel_id=1, source_target_pairs={{0,1},{1,0},{2,3},{3,2},{4,5},{5,4},{6,7},{7,6},{8,9},{9,8},{10,11... | collective-permute-start | bytes 3145736 | tf_op jit(solution)/shard_map/ppermute | solution.py:498
  85.7 35.5 %collective-permute-start.5 = (f16[256,2048]{1,0:T(8,128)(2,1)S(1)}, f16[256,2048]{1,0:T(8,128)(2,1)}, u32[]{:S(2)}, u32[]{:S(2)}) collective-permute-start(f16[256,2048]{1,0:T(8,128)(2,1)S(1)} %convert_element_type.50), channel_id=1, source_target_pairs={{0,1},{1,0},{2,3},{3,2},{4,5},{5,4},{6,7},{7,6},{8,9},{9,8},{10,11... | collective-permute-start | bytes 3145736 | tf_op jit(solution)/shard_map/ppermute | solution.py:498
  110.7 57.9 %all-to-all-start.1 = ((f16[16,2,2,128,128]{4,3,2,1,0:T(8,128)(2,1)}), f16[16,2,2,128,128]{4,3,2,1,0:T(8,128)(2,1)S(1)}, u32[]{:S(2)}, u32[]{:S(2)}) async-start(f16[16,2,2,128,128]{4,3,2,1,0:T(8,128)(2,1)} %convert_element_type.54), calls=%async_computation.1 | async-start | bytes 4194304 | tf_op jit(solution)/shard_map/all_to_all | solution.py:507
  168.6 52.4 %all-to-all-start = ((f16[16,2,2,128,128]{4,3,2,1,0:T(8,128)(2,1)}), f16[16,2,2,128,128]{4,3,2,1,0:T(8,128)(2,1)}, u32[]{:S(2)}, u32[]{:S(2)}) async-start(f16[16,2,2,128,128]{4,3,2,1,0:T(8,128)(2,1)} %convert_element_type.52), calls=%async_computation | async-start | bytes 4194304 | tf_op jit(solution)/shard_map/all_to_all | solution.py:507

commit v4 on v3

--- a/solution.py
+++ b/solution.py
@@ -167,7 +167,7 @@
             divs[k][:, outs] = (divs[k][:, outs] + part[mine]) * 0.5
         return carry
 
-    lax.fori_loop(0, width // 256, second, 0)
+    lax.fori_loop(0, width // 256, second, 0, unroll=2)
 
 
 def stencil(state, heights, flag, xlo, xhi, yl, yr):
@@ -351,7 +351,7 @@
                     ]
         return carry
 
-    lax.fori_loop(0, RADIX, multiply, 0)
+    lax.fori_loop(0, RADIX, multiply, 0, unroll=4)
 
 
 def transform_y(f, twiddle, matrix, groups, each):
@@ -406,7 +406,7 @@
             wide[part, pl.ds(t, inner, stride=count), :] = got[part * inner : (part + 1) * inner]
         return carry
 
-    lax.fori_loop(0, count, multiply, 0)
+    lax.fori_loop(0, count, multiply, 0, unroll=4)
 
     def turn(c, carry):
         block = pl.ds(pl.multiple_of(c * 256, 256), 256)
@@ -414,7 +414,7 @@
             out[part, :, block] = wide[part, block, :].T[: out.shape[1]]
         return carry
 
-    lax.fori_loop(0, wide.shape[1] // 256, turn, 0)
+    lax.fori_loop(0, wide.shape[1] // 256, turn, 0, unroll=4)
 
 
 def transform_x(z, twiddle, matrix, level, levels, earlier):

time: 244 us -> 237 us (0.971)
  Pallas kernels: 109 us -> 96.4 us
  waiting for transfers between devices: 74.8 us -> 80.7 us
    pallas_call x2, Pallas kernels: 36.8 us -> 31 us  [transform_x(): pl.pallas_call(x_kernel, out_shape=jax.ShapeDtypeStruct((2, levels, waves...]
    all_to_all x2, waiting for transfers between devices: 50.6 us -> 56.4 us  [body(): lax.all_to_all(waves.astype(SEND), 'gx', split_axis=0, concat_axis=0, til...]
    pallas_call x2, Pallas kernels: 30.6 us -> 24.8 us  [transform_y(): pl.pallas_call(functools.partial(y_kernel, inner, groups, each), out_shap...]
  transfers between devices with their start and end apart: 8 -> 8, of which waited for: 6 -> 6; matrix products, arithmetic and copies ran while one was open for 10% -> 11% of each run, Pallas kernels for 20% -> 17%
where the time goes in v4:
time: 237 us; the launch traced here: 236 us
  Pallas kernels  96.4 us (41%)
  waiting for transfers between devices  80.7 us (34%)
  other arithmetic  29.3 us (12%)
  starting transfers between devices  21.6 us (9%)
  local copies, waits for them, and re-layouts  7.48 us (3%)
    all_to_all x2, waiting for transfers between devices, body(): lax.all_to_all(waves.astype(SEND), 'gx', split_axis=0, concat_axis=0, til...  56.4 us
    pallas_call x1, Pallas kernels, stencil(): pl.pallas_call(functools.partial(stencil_kernel, bx, width), grid=(length...  40.6 us
    pallas_call x2, Pallas kernels, transform_x(): pl.pallas_call(x_kernel, out_shape=jax.ShapeDtypeStruct((2, levels, waves...  31 us
    pallas_call x2, Pallas kernels, transform_y(): pl.pallas_call(functools.partial(y_kernel, inner, groups, each), out_shap...  24.8 us
    ppermute x2, waiting for transfers between devices, body(): other = lax.ppermute(own, 'gy', swap)  18.6 us
    all_to_all x2, starting transfers between devices, body(): lax.all_to_all(waves.astype(SEND), 'gx', split_axis=0, concat_axis=0, til...  15.4 us
    convert_element_type x2, other arithmetic, body(): waves.astype(SEND)  8.08 us
    convert_element_type x2, other arithmetic, body(): moved.astype(F32)  6.24 us
  transfers between devices with their start and end apart: 8, of which 6 were waited for; matrix products, arithmetic and copies ran while one was open for 11% of the time, Pallas kernels for 17%

profile of v4, /device:TPU:13, one launch (start us, length us, event | category | flops | bytes accessed | tf_op | source)
XLA Modules:
  0.0 236.2 jit_solution(9380907989257104682)
XLA Ops:
  0.6 1.1 fusion.1
  1.7 1.7 convert.6
  3.5 1.9 collective-permute-start
  5.5 1.4 fusion
  7.7 1.4 collective-permute-done.xlo
  9.4 3.2 %collective-permute-done.1.xhi = bf16[9,8,2048]{2,1,0:T(8,128)(2,1)S(1)} collective-permute-done((bf16[9,8,2048]{2,1,0:T(8,128)(2,1)S(1)}, bf16[9,8,2048]{2,1,0:T(8,128)(2,1)S(1)}, u32[]{:S(2)}, u32[]{:S(2)}) %collective-permute-start.1) | collective-permute-done | bytes 294944 | tf_op jit(solution)/shard_map/ppermute | solution.py:466
  13.1 1.3 collective-permute-start.3
  14.7 1.1 collective-permute-done.3
  16.2 1.0 pad.9.yr
  17.6 1.1 pad.8.yl
  18.7 40.6 %stencil.1 = (bf16[4,2,256,2048]{3,2,1,0:T(8,128)(2,1)}, f32[256,2048]{1,0:T(8,128)}, f32[256,2048]{1,0:T(8,128)}) custom-call(bf16[4,2,256,2048]{3,2,1,0:T(8,128)(2,1)} %nxt.1, bf16[4,2,256,2048]{3,2,1,0:T(8,128)(2,1)} %nxt.1, bf16[4,2,256,2048]{3,2,1,0:T(8,128)(2,1)} %nxt.1, s32[256,2048]{1,0:T(8,128)} %h_next.1, s32[256,2048]{1,0:T(8,128)} %h_next.1, ...), custom_call_target="tpu_custom_call" | custom-call | tf_op jit(solution)/shard_map/stencil/pallas_call | solution.py:187
  59.3 2.8 %convert_element_type.48 = f16[256,2048]{1,0:T(8,128)(2,1)} convert(f32[256,2048]{1,0:T(8,128)} %get-tuple-element.9) | non-fusion elementwise | flops 524288 | bytes 3145728 | tf_op jit(solution)/shard_map/convert_element_type | solution.py:494
  62.1 1.2 collective-permute-start.4
  63.9 1.7 convert_element_type.50
  65.7 18.6 %collective-permute-done.4 = f16[256,2048]{1,0:T(8,128)(2,1)} collective-permute-done((f16[256,2048]{1,0:T(8,128)(2,1)}, f16[256,2048]{1,0:T(8,128)(2,1)}, u32[]{:S(2)}, u32[]{:S(2)}) %collective-permute-start.4) | collective-permute-done | bytes 1048608 | tf_op jit(solution)/shard_map/ppermute | solution.py:498
  84.3 1.5 collective-permute-start.5
  85.8 1.7 select_bitcast_fusion.3
  87.5 2.5 %maximum_convert_fusion.f = f32[2,256,2048]{2,1,0:T(8,128)} fusion(f16[1,256,2048]{2,1,0:T(8,128)(2,1)S(1)} %get-tuple-element.21, f16[1,256,2048]{2,1,0:T(8,128)(2,1)S(1)} %get-tuple-element.20), kind=kLoop, calls=%fused_computation | loop fusion | flops 2097152 | bytes 6291456 | tf_op jit(solution)/shard_map/convert_element_type | solution.py:506
  90.0 12.4 %transform_y.2 = f32[16,2,2,128,128]{4,3,2,1,0:T(8,128)} custom-call(f32[2,256,2048]{2,1,0:T(8,128)} %maximum_convert_fusion.f, f32[2,16,256]{2,1,0:T(8,128)} %dynamic-slice_bitcast_fusion.tw, bf16[512,512]{1,0:T(8,128)(2,1)} %constant.34.clone.w), custom_call_target="tpu_custom_call" | custom-call | flops 99999997952 | bytes 10000000 | tf_op jit(solution)/shard_map/transform_y/pallas_call | solution.py:360
  102.4 4.0 %convert_element_type.54 = f16[16,2,2,128,128]{4,3,2,1,0:T(8,128)(2,1)} convert(f32[16,2,2,128,128]{4,3,2,1,0:T(8,128)} %transform_y.2) | non-fusion elementwise | flops 1048576 | bytes 6291456 | tf_op jit(solution)/shard_map/convert_element_type | solution.py:507
  106.5 10.5 %all-to-all-start.1 = ((f16[16,2,2,128,128]{4,3,2,1,0:T(8,128)(2,1)}), f16[16,2,2,128,128]{4,3,2,1,0:T(8,128)(2,1)S(1)}, u32[]{:S(2)}, u32[]{:S(2)}) async-start(f16[16,2,2,128,128]{4,3,2,1,0:T(8,128)(2,1)} %convert_element_type.54), calls=%async_computation.1 | async-start | bytes 4194304 | tf_op jit(solution)/shard_map/all_to_all | solution.py:507
  116.9 1.8 select_bitcast_fusion.1
  118.7 2.5 %maximum_convert_fusion.1.f = f32[2,256,2048]{2,1,0:T(8,128)} fusion(f16[1,256,2048]{2,1,0:T(8,128)(2,1)S(1)} %get-tuple-element.19, f16[1,256,2048]{2,1,0:T(8,128)(2,1)S(1)} %get-tuple-element.18), kind=kLoop, calls=%fused_computation.1 | loop fusion | flops 2097152 | bytes 6291456 | tf_op jit(solution)/shard_map/convert_element_type | solution.py:506
  121.2 12.4 %transform_y.3 = f32[16,2,2,128,128]{4,3,2,1,0:T(8,128)} custom-call(f32[2,256,2048]{2,1,0:T(8,128)} %maximum_convert_fusion.1.f, f32[2,16,256]{2,1,0:T(8,128)} %dynamic-slice_bitcast_fusion.tw, bf16[512,512]{1,0:T(8,128)(2,1)} %constant.34.clone.w), custom_call_target="tpu_custom_call" | custom-call | flops 99999997952 | bytes 10000000 | tf_op jit(solution)/shard_map/transform_y/pallas_call | solution.py:360
  133.6 4.0 %convert_element_type.52 = f16[16,2,2,128,128]{4,3,2,1,0:T(8,128)(2,1)} convert(f32[16,2,2,128,128]{4,3,2,1,0:T(8,128)} %transform_y.3) | non-fusion elementwise | flops 1048576 | bytes 6291456 | tf_op jit(solution)/shard_map/convert_element_type | solution.py:507
  137.7 26.7 %all-to-all-done.1 = f16[16,2,2,128,128]{4,3,2,1,0:T(8,128)(2,1)S(1)} async-done(((f16[16,2,2,128,128]{4,3,2,1,0:T(8,128)(2,1)}), f16[16,2,2,128,128]{4,3,2,1,0:T(8,128)(2,1)S(1)}, u32[]{:S(2)}, u32[]{:S(2)}) %all-to-all-start.1) | async-done | bytes 2097184 | tf_op jit(solution)/shard_map/all_to_all | solution.py:507
  164.3 4.9 %all-to-all-start = ((f16[16,2,2,128,128]{4,3,2,1,0:T(8,128)(2,1)}), f16[16,2,2,128,128]{4,3,2,1,0:T(8,128)(2,1)}, u32[]{:S(2)}, u32[]{:S(2)}) async-start(f16[16,2,2,128,128]{4,3,2,1,0:T(8,128)(2,1)} %convert_element_type.52), calls=%async_computation | async-start | bytes 4194304 | tf_op jit(solution)/shard_map/all_to_all | solution.py:507
  169.2 2.3 convert_element_type.55.z
  171.6 15.5 %transform_x.2.rest_0_ = f32[2,2,128,4096]{3,2,1,0:T(8,128)} custom-call(f32[16,2,2,128,128]{4,3,2,1,0:T(8,128)} %convert_element_type.55.z, f32[2,16,256]{2,1,0:T(8,128)} %constant.35.clone.tw, bf16[1024,512]{1,0:T(8,128)(2,1)} %constant.36.clone.v), custom_call_target="tpu_custom_call" | custom-call | flops 99999997952 | bytes 10000000 | tf_op jit(solution)/shard_map/transform_x/pallas_call | solution.py:425
  187.0 29.7 %all-to-all-done = f16[16,2,2,128,128]{4,3,2,1,0:T(8,128)(2,1)} async-done(((f16[16,2,2,128,128]{4,3,2,1,0:T(8,128)(2,1)}), f16[16,2,2,128,128]{4,3,2,1,0:T(8,128)(2,1)}, u32[]{:S(2)}, u32[]{:S(2)}) %all-to-all-start) | async-done | bytes 2097184 | tf_op jit(solution)/shard_map/all_to_all | solution.py:507
  216.8 3.9 %convert_element_type.53.z = f32[16,2,2,128,128]{4,3,2,1,0:T(8,128)} convert(f16[16,2,2,128,128]{4,3,2,1,0:T(8,128)(2,1)} %all-to-all-done) | non-fusion elementwise | flops 1048576 | bytes 6291456 | tf_op jit(solution)/shard_map/convert_element_type | solution.py:509
  220.7 15.5 %transform_x.3 = f32[2,2,128,4096]{3,2,1,0:T(8,128)} custom-call(f32[16,2,2,128,128]{4,3,2,1,0:T(8,128)} %convert_element_type.53.z, f32[2,16,256]{2,1,0:T(8,128)} %constant.35.clone.tw, bf16[1024,512]{1,0:T(8,128)(2,1)} %constant.36.clone.v, f32[2,2,128,4096]{3,2,1,0:T(8,128)} %transform_x.2.rest_0_), custom_call_target="tpu_custom_call", output_to_operand_aliasing={{}: (3, {})} | custom-call | flops 99999997952 | bytes 10000000 | tf_op jit(solution)/shard_map/transform_x/pallas_call | solution.py:425
  (31 shorter events, 3.6 us)
Async XLA Ops:
  3.5 5.6 %collective-permute-start = (bf16[9,8,2048]{2,1,0:T(8,128)(2,1)S(1)}, bf16[9,8,2048]{2,1,0:T(8,128)(2,1)S(1)}, u32[]{:S(2)}, u32[]{:S(2)}) collective-permute-start(bf16[9,8,2048]{2,1,0:T(8,128)(2,1)S(1)} %pad_maximum_fusion), channel_id=1, source_target_pairs={{0,2},{2,4},{4,6},{6,8},{8,10},{10,12},{12,14},{14,16},{16,18},{18... | collective-permute-start | bytes 884744 | tf_op jit(solution)/shard_map/ppermute | solution.py:466
  5.4 7.2 %collective-permute-start.1 = (bf16[9,8,2048]{2,1,0:T(8,128)(2,1)S(1)}, bf16[9,8,2048]{2,1,0:T(8,128)(2,1)S(1)}, u32[]{:S(2)}, u32[]{:S(2)}) collective-permute-start(bf16[9,8,2048]{2,1,0:T(8,128)(2,1)S(1)} %pad_maximum_fusion.1), channel_id=1, source_target_pairs={{2,0},{4,2},{6,4},{8,6},{10,8},{12,10},{14,12},{16,14},{18,16},{20... | collective-permute-start | bytes 884744 | tf_op jit(solution)/shard_map/ppermute | solution.py:466
  9.1 9.6 %copy-start.1 = (bf16[9,8,2048]{2,1,0:T(8,128)(2,1)}, bf16[9,8,2048]{2,1,0:T(8,128)(2,1)S(1)}, u32[]{:S(2)}) copy-start(bf16[9,8,2048]{2,1,0:T(8,128)(2,1)S(1)} %collective-permute-done.xlo) | copy-start | bytes 884740
  12.6 6.1 %copy-start.2 = (bf16[9,8,2048]{2,1,0:T(8,128)(2,1)}, bf16[9,8,2048]{2,1,0:T(8,128)(2,1)S(1)}, u32[]{:S(2)}) copy-start(bf16[9,8,2048]{2,1,0:T(8,128)(2,1)S(1)} %collective-permute-done.1.xhi) | copy-start | bytes 884740
  13.1 2.8 %collective-permute-start.3 = (bf16[9,272,4]{1,2,0:T(4,128)(2,1)S(1)}, bf16[9,272,4]{1,2,0:T(4,128)(2,1)S(1)}, u32[]{:S(2)}, u32[]{:S(2)}) collective-permute-start(bf16[9,272,4]{1,2,0:T(4,128)(2,1)S(1)} %pad_maximum_fusion.3), channel_id=1, source_target_pairs={{1,0},{0,1},{3,2},{2,3},{5,4},{4,5},{7,6},{6,7},{9,8},{8,9},{11,10... | collective-permute-start | bytes 58760 | tf_op jit(solution)/shard_map/ppermute | solution.py:466
  14.4 2.8 %collective-permute-start.2 = (bf16[9,272,4]{1,2,0:T(4,128)(2,1)S(1)}, bf16[9,272,4]{1,2,0:T(4,128)(2,1)S(1)}, u32[]{:S(2)}, u32[]{:S(2)}) collective-permute-start(bf16[9,272,4]{1,2,0:T(4,128)(2,1)S(1)} %pad_maximum_fusion.2), channel_id=1, source_target_pairs={{0,1},{1,0},{2,3},{3,2},{4,5},{5,4},{6,7},{7,6},{8,9},{9,8},{10,11... | collective-permute-start | bytes 58760 | tf_op jit(solution)/shard_map/ppermute | solution.py:466
  59.3 4.0 %copy-start.3 = (f32[2,2,16,256]{3,2,1,0:T(8,128)S(1)}, f32[2,2,16,256]{3,2,1,0:T(8,128)}, u32[]{:S(2)}) copy-start(f32[2,2,16,256]{3,2,1,0:T(8,128)} %constant.33.clone) | copy-start | bytes 196612
  62.1 23.7 %copy-start = (f32[256,2048]{1,0:T(8,128)S(1)}, f32[256,2048]{1,0:T(8,128)}, u32[]{:S(2)}) copy-start(f32[256,2048]{1,0:T(8,128)} %get-tuple-element.9) | copy-start | bytes 6291460
  62.1 22.2 %collective-permute-start.4 = (f16[256,2048]{1,0:T(8,128)(2,1)}, f16[256,2048]{1,0:T(8,128)(2,1)}, u32[]{:S(2)}, u32[]{:S(2)}) collective-permute-start(f16[256,2048]{1,0:T(8,128)(2,1)} %convert_element_type.48), channel_id=1, source_target_pairs={{0,1},{1,0},{2,3},{3,2},{4,5},{5,4},{6,7},{7,6},{8,9},{9,8},{10,11... | collective-permute-start | bytes 3145736 | tf_op jit(solution)/shard_map/ppermute | solution.py:498
  84.3 32.6 %collective-permute-start.5 = (f16[256,2048]{1,0:T(8,128)(2,1)S(1)}, f16[256,2048]{1,0:T(8,128)(2,1)}, u32[]{:S(2)}, u32[]{:S(2)}) collective-permute-start(f16[256,2048]{1,0:T(8,128)(2,1)S(1)} %convert_element_type.50), channel_id=1, source_target_pairs={{0,1},{1,0},{2,3},{3,2},{4,5},{5,4},{6,7},{7,6},{8,9},{9,8},{10,11... | collective-permute-start | bytes 3145736 | tf_op jit(solution)/shard_map/ppermute | solution.py:498
  106.5 57.9 %all-to-all-start.1 = ((f16[16,2,2,128,128]{4,3,2,1,0:T(8,128)(2,1)}), f16[16,2,2,128,128]{4,3,2,1,0:T(8,128)(2,1)S(1)}, u32[]{:S(2)}, u32[]{:S(2)}) async-start(f16[16,2,2,128,128]{4,3,2,1,0:T(8,128)(2,1)} %convert_element_type.54), calls=%async_computation.1 | async-start | bytes 4194304 | tf_op jit(solution)/shard_map/all_to_all | solution.py:507
  164.3 52.4 %all-to-all-start = ((f16[16,2,2,128,128]{4,3,2,1,0:T(8,128)(2,1)}), f16[16,2,2,128,128]{4,3,2,1,0:T(8,128)(2,1)}, u32[]{:S(2)}, u32[]{:S(2)}) async-start(f16[16,2,2,128,128]{4,3,2,1,0:T(8,128)(2,1)} %convert_element_type.52), calls=%async_computation | async-start | bytes 4194304 | tf_op jit(solution)/shard_map/all_to_all | solution.py:507
